TPU v7x, 32 devices: a whole 2x2x4 slice. The times are simulated.
32 devices in a mesh: dp: 8 (over z, x), seq: 4 (over y, core).
Axes of the slice: x: 2, y: 2, z: 4, core: 2. Of those that a mesh axis runs over, the one named last changes fastest.
Arguments:
- tokens: bfloat16 [88, 360, 768], P('dp', 'seq'), may hold values from -6 to 6
- key_mask: int32 [88, 360], P('dp'), may hold values from 0 to 1, as said below
- row_split: int32 [88, 4], P('dp'), may hold values from 4 to 5, as said below
- group_tags: int32 [88], P('dp'), may hold values from 0 to 8, as said below
- norm1_gain: bfloat16 [768], replicated, may hold values from 0.5 to 1.5
- norm1_shift: bfloat16 [768], replicated, may hold values from -1.796875 to 1.796875
- qkv_weight: bfloat16 [768, 2304], replicated, may hold values from -0.21875 to 0.21875
- query_bias: bfloat16 [768], replicated, may hold values from -1.796875 to 1.796875
- value_bias: bfloat16 [768], replicated, may hold values from -1.796875 to 1.796875
- out_weight: bfloat16 [768, 768], replicated, may hold values from -0.875 to 0.875
- out_bias: bfloat16 [768], replicated, may hold values from -1.796875 to 1.796875
- norm2_gain: bfloat16 [768], replicated, may hold values from 0.5 to 1.5
- norm2_shift: bfloat16 [768], replicated, may hold values from -1.796875 to 1.796875
- fc1_weight: bfloat16 [768, 3072], replicated, may hold values from -0.21875 to 0.21875
- fc1_bias: bfloat16 [3072], replicated, may hold values from -1.796875 to 1.796875
- fc2_weight: bfloat16 [3072, 768], replicated, may hold values from -0.109375 to 0.109375
- fc2_bias: bfloat16 [768], replicated, may hold values from -1.796875 to 1.796875
- out_cotangent: bfloat16 [88, 360, 768], P('dp', 'seq'), may hold values from -6 to 6
Outputs:
- output: bfloat16 [88, 360, 768], P('dp', 'seq')
- input_grad: bfloat16 [88, 360, 768], P('dp', 'seq')
- norm1_gain_grad: float32 [768], P(('dp', 'seq'))
- norm1_shift_grad: float32 [768], P(('dp', 'seq'))
- qkv_weight_grad: float32 [768, 2304], P(None, ('dp', 'seq'))
- query_bias_grad: float32 [768], P(('dp', 'seq'))
- value_bias_grad: float32 [768], P(('dp', 'seq'))
- out_weight_grad: float32 [768, 768], P(None, ('dp', 'seq'))
- out_bias_grad: float32 [768], P(('dp', 'seq'))
- norm2_gain_grad: float32 [768], P(('dp', 'seq'))
- norm2_shift_grad: float32 [768], P(('dp', 'seq'))
- fc1_weight_grad: float32 [768, 3072], P(None, ('dp', 'seq'))
- fc1_bias_grad: float32 [3072], P(('dp', 'seq'))
- fc2_weight_grad: float32 [3072, 768], P(None, ('dp', 'seq'))
- fc2_bias_grad: float32 [768], P(('dp', 'seq'))
Inputs may be any that keep to these rules, and one draw needn't show every extreme that they name: `row_split`: each image's rows sum to 18; every index of seq holds 4 or one more rows, and which indices hold one more differs from image to image. key_mask is 0 on every slot beyond an index's live rows; the first slot of every index of seq is 1 for every image. `group_tags`: the image slots on index g of dp carry tag g or 8; the number of tagged slots differs from index to index, and in every draw one index has all 11 slots tagged.
All inputs are finite; a program needn't handle non-finite values.
Results may differ from a plain program's by a relative error of at most 0.015.
Values may be sent and summed in bfloat16 or wider, within the bound.
No kernel may reach another device: no remote copies, remote signals or barrier semaphores. Data moves between devices by JAX's collectives and lax.ppermute only.
A program may use at most 192 MiB of HBM per device.

v0:
```python
import jax
import jax.numpy as jnp
from jax import lax
from jax.sharding import PartitionSpec as P

HEADS = 12
GRID = 18


EPS = 1e-06
NEG = -1e30


def norm_rows(values, gain, shift):
    row_mean = jnp.mean(values, -1, keepdims=True)
    centered = values - row_mean
    variance = jnp.mean(centered * centered, -1, keepdims=True)
    return centered * lax.rsqrt(variance + EPS) * gain + shift


def exact_gelu(values):
    return jax.nn.gelu(values, approximate=False)


def per_device(
    tokens,
    key_mask,
    row_split,
    group_tags,
    norm1_gain,
    norm1_shift,
    qkv_weight,
    query_bias,
    value_bias,
    out_weight,
    out_bias,
    norm2_gain,
    norm2_shift,
    fc1_weight,
    fc1_bias,
    fc2_weight,
    fc2_bias,
    out_cotangent,
):
    images, slots, width = tokens.shape
    head_dim = width // HEADS
    score_scale = head_dim ** (-0.5)
    seq_count = lax.axis_size("seq")
    group_count = lax.axis_size("dp")
    seq_rank = lax.axis_index("seq")
    rows_here = jnp.sum(jnp.where(jnp.arange(seq_count)[None, :] == seq_rank, row_split, 0), 1)
    row_live = (
        (jnp.arange(slots)[None, :] < (rows_here * GRID)[:, None])
        & (group_tags < group_count)[:, None]
    ).astype(jnp.float32)[..., None]
    key_valid = key_mask > 0
    gain_one = norm1_gain.astype(jnp.float32)
    shift_one = norm1_shift.astype(jnp.float32)
    gain_two = norm2_gain.astype(jnp.float32)
    shift_two = norm2_shift.astype(jnp.float32)
    inputs = tokens.astype(jnp.float32)
    normed = norm_rows(inputs, gain_one, shift_one).astype(jnp.bfloat16)
    projected = jnp.einsum("isd,de->ise", normed, qkv_weight, preferred_element_type=jnp.float32)
    queries = (projected[..., :width] + query_bias.astype(jnp.float32)).astype(jnp.bfloat16)
    key_values = jnp.concatenate(
        [
            projected[..., width : 2 * width],
            projected[..., 2 * width :] + value_bias.astype(jnp.float32),
        ],
        -1,
    ).astype(jnp.bfloat16)
    query_heads = queries.reshape(images, slots, HEADS, head_dim)

    def split_heads(block_kv):
        block_len = block_kv.shape[1]
        return (
            block_kv[..., :width].reshape(images, block_len, HEADS, head_dim),
            block_kv[..., width:].reshape(images, block_len, HEADS, head_dim),
        )

    def block_scores(key_heads):
        return (
            jnp.einsum(
                "iqhe,ikhe->ihqk", query_heads, key_heads, preferred_element_type=jnp.float32
            )
            * score_scale
        )

    run_top = jnp.full((images, HEADS, slots), NEG, jnp.float32)
    key_heads, value_heads = split_heads(lax.all_gather(key_values, "seq", axis=1, tiled=True))
    scores = block_scores(key_heads)
    valid = key_valid[:, None, None, :]
    new_top = jnp.maximum(run_top, jnp.max(jnp.where(valid, scores, NEG), -1))
    exp_terms = jnp.where(valid, jnp.exp(scores - new_top[..., None]), 0.0)
    new_total = jnp.sum(exp_terms, -1)
    new_sum = jnp.einsum(
        "ihqk,ikhe->ihqe",
        exp_terms.astype(jnp.bfloat16),
        value_heads,
        preferred_element_type=jnp.float32,
    )
    mixed = (new_sum / new_total[..., None]).transpose(0, 2, 1, 3)
    log_total = new_top + jnp.log(new_total)
    mixed_low = mixed.reshape(images, slots, width).astype(jnp.bfloat16)
    attended = jnp.einsum(
        "isd,de->ise", mixed_low, out_weight, preferred_element_type=jnp.float32
    ) + out_bias.astype(jnp.float32)
    hidden = inputs + row_live * attended
    normed_two = norm_rows(hidden, gain_two, shift_two).astype(jnp.bfloat16)
    expanded = jnp.einsum(
        "isd,df->isf", normed_two, fc1_weight, preferred_element_type=jnp.float32
    ) + fc1_bias.astype(jnp.float32)
    activated = exact_gelu(expanded).astype(jnp.bfloat16)
    reduced = jnp.einsum(
        "isf,fd->isd", activated, fc2_weight, preferred_element_type=jnp.float32
    ) + fc2_bias.astype(jnp.float32)
    output = (hidden + row_live * reduced).astype(jnp.bfloat16)
    grad_out = out_cotangent.astype(jnp.float32)
    grad_reduced = (row_live * grad_out).astype(jnp.bfloat16)
    fc2_grad = jnp.einsum(
        "isf,isd->fd", activated, grad_reduced, preferred_element_type=jnp.float32
    )
    fc2_bias_grad = jnp.sum(grad_reduced.astype(jnp.float32), (0, 1))
    grad_active = jnp.einsum(
        "isd,fd->isf", grad_reduced, fc2_weight, preferred_element_type=jnp.float32
    ).astype(jnp.bfloat16)
    unused_gelu, gelu_back = jax.vjp(exact_gelu, expanded)
    grad_expanded = gelu_back(grad_active.astype(jnp.float32))[0].astype(jnp.bfloat16)
    fc1_grad = jnp.einsum(
        "isd,isf->df", normed_two, grad_expanded, preferred_element_type=jnp.float32
    )
    fc1_bias_grad = jnp.sum(grad_expanded.astype(jnp.float32), (0, 1))
    grad_normed_two = jnp.einsum(
        "isf,df->isd", grad_expanded, fc1_weight, preferred_element_type=jnp.float32
    )
    unused_norm, norm_two_back = jax.vjp(norm_rows, hidden, gain_two, shift_two)
    grad_hidden_norm, norm2_gain_grad, norm2_shift_grad = norm_two_back(grad_normed_two)
    grad_hidden = grad_out + grad_hidden_norm
    grad_attended = (row_live * grad_hidden).astype(jnp.bfloat16)
    out_grad = jnp.einsum(
        "isd,ise->de", mixed_low, grad_attended, preferred_element_type=jnp.float32
    )
    out_bias_grad = jnp.sum(grad_attended.astype(jnp.float32), (0, 1))
    grad_mixed = jnp.einsum(
        "ise,de->isd", grad_attended, out_weight, preferred_element_type=jnp.float32
    ).astype(jnp.bfloat16)
    grad_heads = grad_mixed.reshape(images, slots, HEADS, head_dim)
    back_kv = lax.all_gather(key_values, "seq", axis=1, tiled=True)
    key_heads, value_heads = split_heads(back_kv)
    scores = block_scores(key_heads)
    valid = key_valid[:, None, None, :]
    weights_back = jnp.where(valid, jnp.exp(scores - log_total[..., None]), 0.0)
    weights_back_low = weights_back.astype(jnp.bfloat16)
    grad_weights = jnp.einsum(
        "iqhe,ikhe->ihqk", grad_heads, value_heads, preferred_element_type=jnp.float32
    )
    row_delta = jnp.sum(weights_back * grad_weights, -1, keepdims=True)
    grad_scores = (weights_back * (grad_weights - row_delta)).astype(jnp.bfloat16)
    query_grad = (
        (
            jnp.einsum(
                "ihqk,ikhe->iqhe", grad_scores, key_heads, preferred_element_type=jnp.float32
            )
            * score_scale
        )
        .reshape(images, slots, width)
        .astype(jnp.bfloat16)
    )
    row_count = slots * lax.axis_size("seq")
    key_part = (
        jnp.einsum("ihqk,iqhe->kihe", grad_scores, query_heads, preferred_element_type=jnp.float32)
        * score_scale
    )
    value_part = jnp.einsum(
        "ihqk,iqhe->kihe", weights_back_low, grad_heads, preferred_element_type=jnp.float32
    )
    kv_summed = lax.psum_scatter(
        jnp.concatenate(
            [
                key_part.reshape(row_count, images, width),
                value_part.reshape(row_count, images, width),
            ],
            -1,
        ).astype(jnp.bfloat16),
        "seq",
        scatter_dimension=0,
        tiled=True,
    )
    kv_grad = kv_summed.transpose(1, 0, 2)
    grad_projected = jnp.concatenate([query_grad, kv_grad], -1)
    qkv_grad = jnp.einsum("isd,ise->de", normed, grad_projected, preferred_element_type=jnp.float32)
    query_bias_grad = jnp.sum(query_grad.astype(jnp.float32), (0, 1))
    value_bias_grad = jnp.sum(kv_grad[..., width:].astype(jnp.float32), (0, 1))
    grad_normed = jnp.einsum(
        "ise,de->isd", grad_projected, qkv_weight, preferred_element_type=jnp.float32
    )
    unused_first, norm_one_back = jax.vjp(norm_rows, inputs, gain_one, shift_one)
    grad_input_norm, norm1_gain_grad, norm1_shift_grad = norm_one_back(grad_normed)
    input_grad = (grad_hidden + grad_input_norm).astype(jnp.bfloat16)
    gain_one_row = norm1_gain_grad[None, :]
    shift_one_row = norm1_shift_grad[None, :]
    query_row = query_bias_grad[None, :]
    value_row = value_bias_grad[None, :]
    out_bias_row = out_bias_grad[None, :]
    gain_two_row = norm2_gain_grad[None, :]
    shift_two_row = norm2_shift_grad[None, :]
    fc1_bias_row = fc1_bias_grad[None, :]
    fc2_bias_row = fc2_bias_grad[None, :]
    summed = (
        lax.psum_scatter(gain_one_row, ("dp", "seq"), scatter_dimension=1, tiled=True),
        lax.psum_scatter(shift_one_row, ("dp", "seq"), scatter_dimension=1, tiled=True),
        lax.psum_scatter(qkv_grad, ("dp", "seq"), scatter_dimension=1, tiled=True),
        lax.psum_scatter(query_row, ("dp", "seq"), scatter_dimension=1, tiled=True),
        lax.psum_scatter(value_row, ("dp", "seq"), scatter_dimension=1, tiled=True),
        lax.psum_scatter(out_grad, ("dp", "seq"), scatter_dimension=1, tiled=True),
        lax.psum_scatter(out_bias_row, ("dp", "seq"), scatter_dimension=1, tiled=True),
        lax.psum_scatter(gain_two_row, ("dp", "seq"), scatter_dimension=1, tiled=True),
        lax.psum_scatter(shift_two_row, ("dp", "seq"), scatter_dimension=1, tiled=True),
        lax.psum_scatter(fc1_grad, ("dp", "seq"), scatter_dimension=1, tiled=True),
        lax.psum_scatter(fc1_bias_row, ("dp", "seq"), scatter_dimension=1, tiled=True),
        lax.psum_scatter(fc2_grad, ("dp", "seq"), scatter_dimension=1, tiled=True),
        lax.psum_scatter(fc2_bias_row, ("dp", "seq"), scatter_dimension=1, tiled=True),
    )
    return (
        output,
        input_grad,
        summed[0][0],
        summed[1][0],
        summed[2],
        summed[3][0],
        summed[4][0],
        summed[5],
        summed[6][0],
        summed[7][0],
        summed[8][0],
        summed[9],
        summed[10][0],
        summed[11],
        summed[12][0],
    )


def solution(mesh):
    return jax.shard_map(
        per_device,
        mesh=mesh,
        in_specs=(
            P("dp", "seq", None),
            P("dp", None),
            P("dp", None),
            P("dp"),
            P(),
            P(),
            P(),
            P(),
            P(),
            P(),
            P(),
            P(),
            P(),
            P(),
            P(),
            P(),
            P(),
            P("dp", "seq", None),
        ),
        out_specs=(
            P("dp", "seq", None),
            P("dp", "seq", None),
            P(("dp", "seq")),
            P(("dp", "seq")),
            P(None, ("dp", "seq")),
            P(("dp", "seq")),
            P(("dp", "seq")),
            P(None, ("dp", "seq")),
            P(("dp", "seq")),
            P(("dp", "seq")),
            P(("dp", "seq")),
            P(None, ("dp", "seq")),
            P(("dp", "seq")),
            P(None, ("dp", "seq")),
            P(("dp", "seq")),
        ),
        check_vma=False,
    )
```

profile of v0, /device:TPU:0, one launch (start us, length us, event | category | flops | bytes accessed | tf_op | source)
XLA Modules:
  0.0 1220.5 jit_solution(15790271560771023204)
XLA Ops:
  10.3 1.7 convert_reduce_fusion.1
  12.1 2.1 fusion.55
  14.8 5.7 fusion.49
  20.7 1.8 fusion.58
  22.8 3.9 copy.56
  30.1 4.0 copy.55
  36.3 106.7 %all-gather.2.cloned.1.call-done = bf16[11,360,1536]{2,0,1:T(8,128)(2,1)} async-done(((bf16[11,90,1536]{2,0,1:T(8,128)(2,1)}), bf16[11,360,1536]{2,0,1:T(8,128)(2,1)}) %all-gather.2.cloned.1.call-update) | async-done | bytes 12165136 | tf_op jit(solution)/shard_map/all_gather | solution.py:90
  143.1 11.9 fusion.91
  154.9 12.4 %copy.87 = bf16[11,360,768]{1,2,0:T(8,128)(2,1)} copy(bf16[11,360,768]{2,0,1:T(8,128)(2,1)} %get-tuple-element.38) | data formatting | bytes 12165120
  167.3 12.3 %copy.88 = bf16[11,360,768]{1,2,0:T(8,128)(2,1)} copy(bf16[11,360,768]{2,0,1:T(8,128)(2,1)} %get-tuple-element.39) | data formatting | bytes 12165120
  179.6 14.2 %select_reduce_fusion = (f32[11,12,90]{2,1,0:T(8,128)S(1)}, f32[11,12,90,360]{3,2,1,0:T(8,128)}) fusion(pred[11,360]{1,0:T(8,128)(4,1)S(1)} %broadcast_compare_fusion, bf16[11,90,12,64]{1,3,2,0:T(8,128)(2,1)} %bitcast.121, bf16[11,360,12,64]{1,3,2,0:T(8,128)(2,1)} %bitcast.118), kind=kOutput, calls=%fused_computation.5 | convolution fusion | flops 560248896 | bytes 24761880 | tf_op jit(solution)/shard_map/iqhe,ikhe->ihqk/dot_general | solution.py:83
  193.9 10.1 fusion
  204.7 11.5 fusion.44
  216.2 1.9 fusion.92
  218.7 11.6 fusion.32
  230.4 31.1 %multiply_convert_fusion.2 = (bf16[11,90,3072]{2,1,0:T(8,128)(2,1)}, f32[11,90,3072]{2,1,0:T(8,128)}) fusion(f32[11,90,3072]{2,1,0:T(8,128)S(1)} %get-tuple-element.47, f32[3072]{0:T(1024)S(1)} %copy-done.33, u16[90,3072]{1,0:T(8,128)(2,1)S(1)} %get-tuple-element.16, u16[90,3072]{1,0:T(8,128)(2,1)S(1)} %get-tuple-element.15), kind=kLoop, calls=%fused_computation.25 | loop fusion | flops 215930880 | bytes 31531008 | tf_op jit(solution)/shard_map/convert_element_type | solution.py:113
  261.5 18.1 %convert_reduce_fusion = (f32[3072]{0:T(1024)}, bf16[11,90,3072]{2,1,0:T(8,128)(2,1)}) fusion(f32[11,90,3072]{2,1,0:T(8,128)} %get-tuple-element.37, bf16[3072,768]{1,0:T(8,128)(2,1)} %param.33, bf16[11,90,768]{2,1,0:T(8,128)(2,1)} %param.35, f32[11,90]{1,0:T(8,128)S(1)} %fusion.71, f32[11,90,3072]{2,1,0:T(8,128)} %copy-done.9, f32[3072]{0:T(1024)} %convert_element_type.136), kind=kOutput, calls=%fused_computation.23 | convolution fusion | flops 4731468288 | bytes 36680568 | tf_op jit(solution)/shard_map/isd,fd->isf/dot_general | solution.py:124
  279.5 11.8 multiply_reduce_fusion.1
  296.9 2.6 convolution_convert_fusion
  299.5 4.0 copy.60
  303.5 11.3 fusion.28
  314.8 17.4 %multiply_reduce_fusion = (f32[11,12,90]{2,1,0:T(8,128)}, f32[11,12,90,360]{3,2,1,0:T(8,128)}) fusion(f32[11,12,90,360]{3,2,1,0:T(8,128)} %get-tuple-element.44, f32[11,12,90]{2,1,0:T(8,128)} %log_add_fusion, pred[11,360]{1,0:T(8,128)(4,1)S(1)} %broadcast_compare_fusion, bf16[11,90,12,64]{1,3,2,0:T(8,128)(2,1)} %bitcast.125, ...), kind=kOutput, calls=%fused_computation.1 | convolution fusion | flops 568802496 | bytes 41916600 | tf_op jit(solution)/shard_map/iqhe,ikhe->ihqk/dot_general | solution.py:154
  332.2 9.4 copy.62
  341.6 16.7 %multiply_convert_fusion = bf16[11,12,90,360]{3,2,1,0:T(8,128)(2,1)S(1)} fusion(f32[11,12,90,360]{3,2,1,0:T(8,128)} %get-tuple-element.50, f32[11,12,90,360]{3,2,1,0:T(8,128)} %get-tuple-element.44, f32[11,12,90]{2,1,0:T(8,128)} %get-tuple-element.49, f32[11,12,90]{2,1,0:T(8,128)} %log_add_fusion, pred[11,360]{1,0:T(8,128)(4,1)S(1)} %broadcast_compare_fusion), kind=kLoop, calls=%fused_computation | loop fusion | flops 25660800 | bytes 42867000 | tf_op jit(solution)/shard_map/convert_element_type | solution.py:158
  358.3 4.5 multiply_convert_fusion.1
  363.9 9.4 copy.61
  373.3 10.6 pad_maximum_fusion
  384.0 2.4 copy.83
  386.5 5.7 convolution_bitcast_fusion.3
  392.2 12.4 %convolution_bitcast_fusion = f32[3072,768]{0,1:T(8,128)} fusion(bf16[11,90,3072]{2,1,0:T(8,128)(2,1)} %get-tuple-element.36, bf16[11,90,768]{2,1,0:T(8,128)(2,1)} %param.35, f32[11,90]{1,0:T(8,128)S(1)} %fusion.71), kind=kOutput, calls=%fused_computation.53 | convolution fusion | flops 4673687040 | bytes 17044344 | tf_op jit(solution)/shard_map/isf,isd->fd/dot_general | solution.py:120
  405.3 12.1 convolution_bitcast_fusion.1
  419.4 12.1 convert_reduce_fusion.2
  431.5 4.3 copy.63
  435.8 162.4 %all-reduce.12.cloned.1.call-done = bf16[360,11,1536]{2,0,1:T(8,128)(2,1)} async-done(((bf16[360,11,1536]{2,0,1:T(8,128)(2,1)}), bf16[360,11,1536]{2,0,1:T(8,128)(2,1)}) %all-reduce.12.cloned.1.call-update) | async-done | bytes 12165136
  598.3 3.0 dynamic-slice_bitcast_fusion
  601.2 1.6 copy-done.11
  602.9 8.2 convolution_bitcast_fusion.2
  618.9 10.2 add_convert_fusion.1
  629.1 72.4 %reduce-scatter.25.cloned.1.call-done = f32[96,1]{1,0:T(8,128)} async-done(((f32[3072,1]{1,0:T(8,128)}), f32[96,1]{1,0:T(8,128)}) %reduce-scatter.25.cloned.1.call-update) | async-done | bytes 400
  702.9 1.7 convert_reduce_fusion.5
  705.2 7.4 fusion.88
  713.2 2.5 fusion.53
  716.4 41.0 %all-reduce.9 = (f32[1,768]{1,0:T(1,128)}, f32[1,768]{1,0:T(1,128)}, f32[1,768]{1,0:T(1,128)}, f32[1,768]{1,0:T(1,128)}, f32[1,768]{1,0:T(1,128)}, /*index=5*/f3...) all-reduce(f32[1,768]{1,0:T(1,128)} %broadcast_in_dim.116, ...), channel_id=3, replica_groups=mesh['dp'=8,'seq'=4] {'dp','seq'}, use_global_device_ids=true, to_apply=%region_14.15.clone | all-reduce | flops 6144 | bytes 49152
  763.1 5.6 add_convert_fusion
  768.8 37.3 %reduce-scatter.19.cloned.1.call-done = f32[768,24]{0,1:T(8,128)} async-done(((f32[768,768]{0,1:T(8,128)}), f32[768,24]{0,1:T(8,128)}) %reduce-scatter.19.cloned.1.call-update) | async-done | bytes 73744 | tf_op jit(solution)/shard_map/reduce_scatter | solution.py:215
  806.1 141.0 %reduce-scatter.23.cloned.1.call-done = f32[3072,24]{0,1:T(8,128)} async-done(((f32[3072,768]{0,1:T(8,128)}), f32[3072,24]{0,1:T(8,128)}) %reduce-scatter.23.cloned.1.call-update) | async-done | bytes 294928 | tf_op jit(solution)/shard_map/reduce_scatter | solution.py:221
  947.0 142.0 %reduce-scatter.21.cloned.1.call-done = f32[768,96]{0,1:T(8,128)} async-done(((f32[768,3072]{0,1:T(8,128)}), f32[768,96]{0,1:T(8,128)}) %reduce-scatter.21.cloned.1.call-update) | async-done | bytes 294928 | tf_op jit(solution)/shard_map/reduce_scatter | solution.py:219
  1089.1 124.4 %reduce-scatter.17.cloned.1.call-done = f32[768,72]{0,1:T(8,128)} async-done(((f32[768,2304]{0,1:T(8,128)}), f32[768,72]{0,1:T(8,128)}) %reduce-scatter.17.cloned.1.call-update) | async-done | bytes 221200 | tf_op jit(solution)/shard_map/reduce_scatter | solution.py:212
  (157 shorter events, 36.5 us)
Async XLA Ops:
  7.2 7.6 copy-start
  7.2 135.9 %all-gather.2.cloned.1.call-start = ((), (), s32[]{:S(2)}) async-start(), calls=%async_computation.5 | async-start | bytes 22118400 | tf_op jit(solution)/shard_map/all_gather | solution.py:90
  8.1 12.4 %copy-start.34 = (f32[768]{0:T(1024)}, f32[768]{0:T(1024)S(1)}, u32[]{:S(2)}) copy-start(f32[768]{0:T(1024)S(1)} %convert_element_type.123) | copy-start | bytes 9220
  9.0 5.8 copy-start.44
  12.1 8.4 copy-start.18
  14.8 5.7 copy-start.20
  22.8 4.2 copy-start.47
  22.8 4.8 copy-start.48
  22.8 6.6 copy-start.43
  26.7 571.6 %all-reduce.12.cloned.1.call-start = ((), (), s32[]{:S(2)}) async-start(), calls=%async_computation.11 | async-start | bytes 24330240
  35.6 356.7 %copy-start.24 = (f32[11,90]{1,0:T(8,128)}, f32[11,90]{1,0:T(8,128)S(1)}, u32[]{:S(2)}) copy-start(f32[11,90]{1,0:T(8,128)S(1)} %fusion.71) | copy-start | bytes 11884
  204.7 11.5 copy-start.2
  204.7 11.5 copy-start.16
  204.7 11.5 copy-start.40
  216.1 2.5 copy-start.13
  216.2 2.5 copy-start.33
  218.1 12.2 %copy-start.7 = (f32[11,90,768]{2,1,0:T(8,128)}, f32[11,90,768]{2,1,0:T(8,128)S(1)}, u32[]{:S(2)}) copy-start(f32[11,90,768]{2,1,0:T(8,128)S(1)} %get-tuple-element.46) | copy-start | bytes 9123844
  218.1 12.2 %copy-start.30 = (f32[11,90]{1,0:T(8,128)}, f32[11,90]{1,0:T(8,128)S(1)}, u32[]{:S(2)}) copy-start(f32[11,90]{1,0:T(8,128)S(1)} %broadcast_multiply_fusion) | copy-start | bytes 11884
  218.7 11.7 copy-start.28
  218.7 11.7 copy-start.37
  230.4 31.1 %copy-start.9 = (f32[11,90,3072]{2,1,0:T(8,128)}, f32[11,90,3072]{2,1,0:T(8,128)S(1)}, u32[]{:S(2)}) copy-start(f32[11,90,3072]{2,1,0:T(8,128)S(1)} %get-tuple-element.47) | copy-start | bytes 36495364
  279.5 11.8 copy-start.29
  279.5 11.8 copy-start.8
  279.5 11.8 copy-start.31
  279.5 11.8 copy-start.38
  279.5 11.8 copy-start.42
  291.4 2.8 copy-start.12
  292.5 4.4 copy-start.17
  292.5 3.2 copy-start.23
  341.6 16.7 %copy-start.5 = (bf16[11,90,768]{1,2,0:T(8,128)(2,1)S(1)}, bf16[11,90,768]{1,2,0:T(8,128)(2,1)}, u32[]{:S(2)}) copy-start(bf16[11,90,768]{1,2,0:T(8,128)(2,1)} %copy.55) | copy-start | bytes 4561924
  358.3 5.6 copy-start.1
  383.9 317.6 %reduce-scatter.25.cloned.1.call-start = ((), (), s32[]{:S(2)}) async-start(), calls=%async_computation.10 | async-start | bytes 1622016
  386.4 419.7 %reduce-scatter.19.cloned.1.call-start = ((), (), s32[]{:S(2)}) async-start(), calls=%async_computation.7 | async-start | bytes 2433024 | tf_op jit(solution)/shard_map/reduce_scatter | solution.py:215
  392.2 554.9 %reduce-scatter.23.cloned.1.call-start = ((), (), s32[]{:S(2)}) async-start(), calls=%async_computation.9 | async-start | bytes 9732096 | tf_op jit(solution)/shard_map/reduce_scatter | solution.py:221
  404.6 684.4 %reduce-scatter.21.cloned.1.call-start = ((), (), s32[]{:S(2)}) async-start(), calls=%async_computation.8 | async-start | bytes 9732096 | tf_op jit(solution)/shard_map/reduce_scatter | solution.py:219
  417.5 796.0 %reduce-scatter.17.cloned.1.call-start = ((), (), s32[]{:S(2)}) async-start(), calls=%async_computation.6 | async-start | bytes 7299072 | tf_op jit(solution)/shard_map/reduce_scatter | solution.py:212
  431.5 171.4 %copy-start.19 = (f32[11,90]{1,0:T(8,128)S(1)}, f32[11,90]{1,0:T(8,128)}, u32[]{:S(2)}) copy-start(f32[11,90]{1,0:T(8,128)} %copy-done.18) | copy-start | bytes 11884
  431.5 171.4 %copy-start.21 = (f32[11,90]{1,0:T(8,128)S(1)}, f32[11,90]{1,0:T(8,128)}, u32[]{:S(2)}) copy-start(f32[11,90]{1,0:T(8,128)} %copy-done.20) | copy-start | bytes 11884
  598.3 4.6 copy-start.3
  598.3 4.6 copy-start.15
  598.3 4.6 copy-start.35
  598.3 4.6 copy-start.45
  611.2 7.8 copy-start.25
  705.2 8.0 copy-start.27
  705.2 8.0 copy-start.4
  705.2 8.0 copy-start.22
  705.2 8.0 copy-start.36
  712.6 3.2 copy-start.10
  (9 other events, 12.2 us)
Sparse Core Ops, SparseCore 0:
  26.8 116.1 all-gather.1
  384.0 214.1 all-reduce.11
  604.4 97.0 reduce-scatter.24
  708.1 97.9 reduce-scatter.18
  812.4 134.5 reduce-scatter.22
  954.4 134.6 reduce-scatter.20
  1095.3 118.1 reduce-scatter.16
where the time goes:
time: 1230 us; the launch traced here: 1220 us
  waiting for transfers between devices  786 us (64%)
  matrix products  179 us (15%)
  local copies, waits for them, and re-layouts  99.9 us (8%)
  other arithmetic  98.6 us (8%)
  blocking collectives  41 us (3%)
  between operations  15.5 us (1%)
    unnamed x9, waiting for transfers between devices  235 us
    reduce_scatter x1, waiting for transfers between devices, per_device(): lax.psum_scatter(fc1_grad, ('dp', 'seq'), scatter_dimension=1, tiled=True)  142 us
    reduce_scatter x1, waiting for transfers between devices, per_device(): lax.psum_scatter(fc2_grad, ('dp', 'seq'), scatter_dimension=1, tiled=True)  141 us
    reduce_scatter x1, waiting for transfers between devices, per_device(): lax.psum_scatter(qkv_grad, ('dp', 'seq'), scatter_dimension=1, tiled=True)  124 us
    all_gather x1, waiting for transfers between devices, per_device(): lax.all_gather(key_values, 'seq', axis=1, tiled=True)  107 us
    unnamed x1, blocking collectives  41 us
    reduce_scatter x1, waiting for transfers between devices, per_device(): lax.psum_scatter(out_grad, ('dp', 'seq'), scatter_dimension=1, tiled=True)  37.3 us
    unnamed x105, local copies, waits for them, and re-layouts  36.6 us
  transfers between devices with their start and end apart: 7, of which 7 were waited for; matrix products, arithmetic and copies ran while one was open for 9% of the time, Pallas kernels for 0%

commit v1 on v0

v1 whole, which is shorter than its diff:
```python
import functools

import jax
import jax.numpy as jnp
from jax import lax
from jax.experimental import pallas as pl
from jax.experimental.pallas import tpu as pltpu
from jax.sharding import PartitionSpec as P

HEADS = 12
GRID = 18
EPS = 1e-06
NEG = -1e30
F32 = jnp.float32
BF16 = jnp.bfloat16
VMEM_LIMIT = 60 * 1024 * 1024
CHUNK = 256


def round_up(n, to):
    return -(-n // to) * to


class Rows:
    def __init__(self, ranks, slots):
        base, extra = GRID // ranks, GRID % ranks
        self.lens = [min(slots, (base + 1) * GRID)] * extra + [base * GRID] * (ranks - extra)
        self.extra = extra
        self.ranks = ranks
        self.slots = slots
        self.offs = []
        at = 0
        for n in self.lens:
            self.offs.append(at)
            at += round_up(n, 8)
        self.rows = round_up(at, 16)
        self.keys = round_up(self.rows, 128)
        self.piece = round_up(slots, 16)
        self.spare = round_up(max(o + round_up(n, 16) for o, n in zip(self.offs, self.lens)), 8) - self.rows
        self.spare = max(self.spare, 0)

    def is_row(self, index):
        hit = None
        for off, n in zip(self.offs, self.lens):
            one = (index >= off) & (index < off + n)
            hit = one if hit is None else hit | one
        return hit


def dot(a, b):
    return lax.dot_general(a, b, (((1,), (0,)), ((), ())), preferred_element_type=F32)


def dot_nt(a, b):
    return lax.dot_general(a, b, (((1,), (1,)), ((), ())), preferred_element_type=F32)


def dot_tn(a, b):
    return lax.dot_general(a, b, (((0,), (0,)), ((), ())), preferred_element_type=F32)


def params(n=0):
    return pltpu.CompilerParams(
        vmem_limit_bytes=VMEM_LIMIT, dimension_semantics=("arbitrary",) * n if n else None
    )


def unpack(lay, stage, scal_ref, base, to_ref, start):
    width = to_ref.shape[1]
    for i, (off, n) in enumerate(zip(lay.offs, lay.lens)):
        full = round_up(n, 8)
        if full > n:
            to_ref[start + off + full - 8 : start + off + full, :] = jnp.zeros((8, width), F32)
        piece = stage[scal_ref[base + i]].astype(F32)
        to_ref[start + off : start + off + n, :] = piece[:n]
    last = lay.offs[-1] + round_up(lay.lens[-1], 8)
    if lay.rows > last:
        to_ref[start + last : start + lay.rows, :] = jnp.zeros((lay.rows - last, width), F32)


def repack(lay, from_ref, start, scal_ref, base, out_ref, lead):
    for i, (off, n) in enumerate(zip(lay.offs, lay.lens)):
        full = round_up(n, 16)
        rows = from_ref[start + off : start + off + full, :].astype(BF16)
        out_ref[(*lead, scal_ref[base + i], slice(0, full), slice(None))] = rows


def live_column(lay, tag):
    index = lax.broadcasted_iota(jnp.int32, (lay.rows, 1), 0)
    return jnp.where(lay.is_row(index), tag, 0).astype(F32)


def normalise(x):
    mean = jnp.mean(x, -1, keepdims=True)
    centered = x - mean
    rstd = lax.rsqrt(jnp.mean(centered * centered, -1, keepdims=True) + EPS)
    return centered * rstd, rstd


def half_masks():
    lane = lax.broadcasted_iota(jnp.int32, (1, 128), 1)
    return [(lane < 64).astype(BF16), (lane >= 64).astype(BF16)]


def attention_forward(
    lay,
    alias,
    scal_ref,
    p0,
    p1,
    p2,
    p3,
    mask_ref,
    vec_ref,
    bias_ref,
    wqkv_ref,
    wout_ref,
    *refs,
):
    hid_ref, x_ref, normed_ref, mixed_ref, qkv_ref, prob_ref, stage, xs = refs[4 if alias else 0 :]
    width = wout_ref.shape[0]
    rows, keys = lay.rows, lay.keys
    for j, piece in enumerate((p0, p1, p2, p3)):
        stage[j] = piece[0]
    unpack(lay, stage, scal_ref, 0, xs, 0)
    x = xs[...]
    x_ref[0] = x.astype(BF16)
    xhat, _ = normalise(x)
    normed_ref[0] = (xhat * vec_ref[0:1] + vec_ref[1:2]).astype(BF16)
    normed = normed_ref[0]
    for c in range(0, 3 * width, CHUNK):
        part = dot(normed, wqkv_ref[:, c : c + CHUNK]) + bias_ref[:, c : c + CHUNK]
        if c < width:
            part = part * 0.125
        qkv_ref[0:rows, c : c + CHUNK] = part.astype(BF16)
    if keys > rows:
        qkv_ref[rows:keys, :] = jnp.zeros((keys - rows, 3 * width), BF16)
    masks = half_masks()

    def pair(p):
        at = pl.multiple_of(p * 128, 128)
        q = qkv_ref[0:rows, pl.ds(at, 128)]
        k = qkv_ref[:, pl.ds(pl.multiple_of(width + at, 128), 128)]
        v = qkv_ref[:, pl.ds(pl.multiple_of(2 * width + at, 128), 128)]
        total = None
        for h in (0, 1):
            s = dot_nt(q, k * masks[h]) + mask_ref[...]
            e = jnp.exp(s - jnp.max(s, -1, keepdims=True))
            prob = (e * (1.0 / jnp.sum(e, -1, keepdims=True))).astype(BF16)
            prob_ref[2 * p + h] = prob
            part = dot(prob, v * masks[h])
            total = part if total is None else total + part
        mixed_ref[0, :, pl.ds(at, 128)] = total.astype(BF16)

    pl.loop(0, width // 128, unroll=2)(pair)
    attended = dot(mixed_ref[0], wout_ref[...]) + vec_ref[2:3]
    hid_ref[0] = xs[...] + live_column(lay, scal_ref[lay.ranks]) * attended


def feed_forward(
    lay,
    per,
    steps,
    scal_ref,
    hid_ref,
    c0,
    c1,
    c2,
    c3,
    w1_ref,
    b1_ref,
    w2_ref,
    vec_ref,
    out_ref,
    gh_ref,
    ga_ref,
    dw1_ref,
    dw2_ref,
    db1_ref,
    dvec_ref,
    stage,
    grad,
    n2,
    gr,
    grt,
    red,
    gn,
    act,
    gexp,
):
    step = pl.program_id(0)
    rows = lay.rows
    each = lay.ranks + 1

    @pl.when(step == 0)
    def _():
        total = None
        for k in range(per):
            block = slice(k * rows, (k + 1) * rows)
            for j, piece in enumerate((c0, c1, c2, c3)):
                stage[j] = piece[k]
            unpack(lay, stage, scal_ref, k * each, grad, k * rows)
            live = live_column(lay, scal_ref[k * each + lay.ranks])
            reduced = (live * grad[block, :]).astype(BF16)
            gr[block, :] = reduced
            wide = reduced.astype(F32)
            grt[:, block] = wide.T.astype(BF16)
            total = jnp.sum(wide, 0, keepdims=True) + (0.0 if total is None else total)
            xhat, _ = normalise(hid_ref[k])
            n2[block, :] = (xhat * vec_ref[0:1] + vec_ref[1:2]).astype(BF16)
        dvec_ref[...] = jnp.zeros_like(dvec_ref)
        dvec_ref[3:4] = total
        red[...] = jnp.zeros_like(red)
        gn[...] = jnp.zeros_like(gn)

    total = None
    for k in range(per):
        block = slice(k * rows, (k + 1) * rows)
        expanded = dot(n2[block, :], w1_ref[...]) + b1_ref[...]
        cdf = 0.5 * (1.0 + lax.erf(expanded * 0.7071067811865476))
        slope = cdf + expanded * (jnp.exp(-0.5 * expanded * expanded) * 0.3989422804014327)
        act[block, :] = (expanded * cdf).astype(BF16)
        grad_active = dot_nt(gr[block, :], w2_ref[...])
        grad_exp = (grad_active * slope).astype(BF16)
        gexp[block, :] = grad_exp
        total = jnp.sum(grad_exp.astype(F32), 0, keepdims=True) + (0.0 if total is None else total)
        red[block, :] += dot(act[block, :], w2_ref[...])
        gn[block, :] += dot_nt(gexp[block, :], w1_ref[...])
    db1_ref[...] = total
    dw1_ref[...] = dot_tn(gexp[...], n2[...]).astype(BF16)
    dw2_ref[...] = dot(grt[...], act[...]).astype(BF16)

    @pl.when(step == steps - 1)
    def _():
        for k in range(per):
            block = slice(k * rows, (k + 1) * rows)
            live = live_column(lay, scal_ref[k * each + lay.ranks])
            hidden = hid_ref[k]
            red[block, :] = hidden + live * (red[block, :] + vec_ref[2:3])
            xhat, rstd = normalise(hidden)
            grad_n2 = gn[block, :]
            dvec_ref[0:1] += jnp.sum(grad_n2 * xhat, 0, keepdims=True)
            dvec_ref[1:2] += jnp.sum(grad_n2, 0, keepdims=True)
            scaled = grad_n2 * vec_ref[0:1]
            row = scaled - jnp.mean(scaled, -1, keepdims=True)
            row = row - xhat * jnp.mean(scaled * xhat, -1, keepdims=True)
            grad_hidden = grad[block, :] + rstd * row
            gh_ref[k] = grad_hidden
            attended = (live * grad_hidden).astype(BF16)
            ga_ref[k] = attended
            dvec_ref[2:3] += jnp.sum(attended.astype(F32), 0, keepdims=True)
        for k in range(per):
            repack(lay, red, k * rows, scal_ref, k * each, out_ref, (k,))


def attention_backward(
    lay,
    alias,
    scal_ref,
    ga_ref,
    gh_ref,
    x_ref,
    qkv_ref,
    prob_ref,
    vec_ref,
    wqkv_ref,
    wout_ref,
    *refs,
):
    ig_ref, gp_ref, dvec_ref, gm_ref, res = refs[1 if alias else 0 :]
    width = wout_ref.shape[0]
    rows = lay.rows
    gm_ref[...] = dot_nt(ga_ref[0], wout_ref[...]).astype(BF16)
    masks = half_masks()

    def pair(p):
        at = pl.multiple_of(p * 128, 128)
        at_k = pl.multiple_of(width + at, 128)
        at_v = pl.multiple_of(2 * width + at, 128)
        q = qkv_ref[0:rows, pl.ds(at, 128)]
        k = qkv_ref[:, pl.ds(at_k, 128)]
        v = qkv_ref[:, pl.ds(at_v, 128)]
        gm = gm_ref[:, pl.ds(at, 128)]
        dq = dk = dv = None
        for h in (0, 1):
            prob = prob_ref[2 * p + h]
            weights = prob.astype(F32)
            gw = dot_nt(gm, v * masks[h])
            delta = jnp.sum(weights * gw, -1, keepdims=True)
            ds = (weights * (gw - delta)).astype(BF16)
            parts = dot(ds, k * masks[h]), dot_tn(ds, q * masks[h]), dot_tn(prob, gm * masks[h])
            if h == 0:
                dq, dk, dv = parts
            else:
                dq, dk, dv = dq + parts[0], dk + parts[1], dv + parts[2]
        gp_ref[0, :, pl.ds(at, 128)] = (dq * 0.125).astype(BF16)
        gp_ref[0, :, pl.ds(at_k, 128)] = dk[:rows].astype(BF16)
        gp_ref[0, :, pl.ds(at_v, 128)] = dv[:rows].astype(BF16)

    pl.loop(0, width // 128, unroll=2)(pair)
    dvec_ref[...] = jnp.zeros_like(dvec_ref)
    dvec_ref[2:3] = jnp.sum(gp_ref[0, :, 0:width].astype(F32), 0, keepdims=True)
    dvec_ref[3:4] = jnp.sum(gp_ref[0, :, 2 * width :].astype(F32), 0, keepdims=True)
    grad_normed = dot_nt(gp_ref[0], wqkv_ref[...])
    xhat, rstd = normalise(x_ref[0].astype(F32))
    dvec_ref[0:1] = jnp.sum(grad_normed * xhat, 0, keepdims=True)
    dvec_ref[1:2] = jnp.sum(grad_normed, 0, keepdims=True)
    scaled = grad_normed * vec_ref[0:1]
    row = scaled - jnp.mean(scaled, -1, keepdims=True)
    row = row - xhat * jnp.mean(scaled * xhat, -1, keepdims=True)
    res[0:rows] = gh_ref[0] + rstd * row
    repack(lay, res, 0, scal_ref, 0, ig_ref, ())


def outer_sum(a_ref, b_ref, out_ref):
    out_ref[...] = dot_tn(a_ref[...], b_ref[...]).astype(BF16)


def weight_sum(a, b, block):
    rows, n = a.shape
    m = b.shape[1]
    return pl.pallas_call(
        outer_sum,
        grid=(n // block,),
        in_specs=[
            pl.BlockSpec((rows, block), lambda i: (0, i)),
            pl.BlockSpec((rows, m), lambda i: (0, 0)),
        ],
        out_specs=pl.BlockSpec((block, m), lambda i: (i, 0)),
        out_shape=jax.ShapeDtypeStruct((n, m), BF16),
        compiler_params=params(1),
        cost_estimate=pl.CostEstimate(
            flops=2 * rows * n * m, bytes_accessed=2 * (rows * (n + m) + n * m), transcendentals=0
        ),
    )(a, b)


def whole(shape):
    return pl.BlockSpec(shape, lambda i: (0,) * len(shape))


def at_image(k, shape):
    return pl.BlockSpec((1, *shape[1:]), lambda i: (k,) + (0,) * (len(shape) - 1))


SMEM = pl.BlockSpec(memory_space=pltpu.SMEM)
HBM = pl.BlockSpec(memory_space=pl.ANY)


class Exchange:
    def __init__(self, n_dp, n_seq):
        self.sizes = (n_dp, n_seq)
        self.bits = []
        for axis, size in (("dp", n_dp), ("seq", n_seq)):
            mask = size // 2
            while mask:
                self.bits.append((axis, mask))
                mask //= 2
        self.n_seq = n_seq

    def order(self, kind):
        names = list(range(len(self.bits)))
        if len(names) != 5:
            return names[::-1]
        z1, z0, x, y, core = names
        return {
            "xyz": [core, x, y, z0, z1],
            "yxz": [core, y, x, z0, z1],
            "zxy": [core, z0, x, z1, y],
            "xzy": [core, x, z0, z1, y],
            "yzx": [core, y, z0, z1, x],
        }[kind]

    def scatter_sum(self, terms, kind, keep=None):
        held = terms.reshape((2,) * len(self.bits) + terms.shape[2:])
        left = list(range(len(self.bits)))
        for bit in self.order(kind):
            axis, mask = self.bits[bit]
            dim = left.index(bit)
            mine = (lax.axis_index(axis) // mask) % 2
            size = self.sizes[0] if axis == "dp" else self.sizes[1]
            other = lax.dynamic_index_in_dim(held, 1 - mine, dim, keepdims=False)
            own = lax.dynamic_index_in_dim(held, mine, dim, keepdims=False)
            got = lax.ppermute(other, axis, [(i, i ^ mask) for i in range(size)])
            left.remove(bit)
            held = own.astype(F32) + got.astype(F32)
            if left:
                held = held.astype(terms.dtype)
        return held


def per_device(
    tokens,
    key_mask,
    row_split,
    group_tags,
    norm1_gain,
    norm1_shift,
    qkv_weight,
    query_bias,
    value_bias,
    out_weight,
    out_bias,
    norm2_gain,
    norm2_shift,
    fc1_weight,
    fc1_bias,
    fc2_weight,
    fc2_bias,
    out_cotangent,
):
    images, slots, width = tokens.shape
    hidden_width = fc1_weight.shape[1]
    n_seq = lax.axis_size("seq")
    n_dp = lax.axis_size("dp")
    rank = lax.axis_index("seq")
    lay = Rows(n_seq, slots)
    per = -(-images // n_seq)
    rows, keys = lay.rows, lay.keys

    def swap(value, j):
        return lax.ppermute(value, "seq", [(i, i ^ j) for i in range(n_seq)])

    def rows_of(array, owner, k):
        return lax.dynamic_slice_in_dim(array, jnp.minimum(owner * per + k, images - 1), 1, 0)

    def bring(array, k):
        return [rows_of(array, rank, k)] + [
            swap(rows_of(array, rank ^ j, k), j) for j in range(1, n_seq)
        ]

    number = rank * per + jnp.arange(per)
    pick = (jnp.minimum(number, images - 1)[:, None] == jnp.arange(images)[None, :]).astype(jnp.int32)
    split_own = jnp.sum(pick[:, :, None] * row_split[None], 1)
    tag_own = jnp.sum(pick * group_tags[None], 1)
    counts = ((tag_own < n_dp) & (number < images)).astype(jnp.int32)
    long = (split_own > GRID // n_seq).astype(jnp.int32)
    earlier = jnp.tril(jnp.ones((n_seq, n_seq), jnp.int32), -1)
    long_before = jnp.sum(long[:, None, :] * earlier[None], -1)
    short_before = jnp.sum((1 - long)[:, None, :] * earlier[None], -1)
    place = jnp.where(long == 1, long_before, lay.extra + short_before)
    hits = (place[:, None, :] == jnp.arange(n_seq)[None, :, None]).astype(jnp.int32)
    source = jnp.sum(hits * jnp.arange(n_seq)[None, None, :], -1)
    scal = jnp.concatenate([source ^ rank, counts[:, None]], 1)
    mask_own = jnp.sum(pick[:, :, None] * key_mask[None], 1).reshape(per, 1, n_seq, slots)
    mask_seg = jnp.sum(hits[..., None] * mask_own, 2)
    mask_rows = []
    for i, n in enumerate(lay.lens):
        end = lay.offs[i + 1] if i + 1 < n_seq else keys
        mask_rows.append(jnp.pad(mask_seg[:, i, :n], ((0, 0), (0, end - lay.offs[i] - n))))
    mask_row = jnp.where(jnp.concatenate(mask_rows, 1) > 0, 0.0, NEG).astype(F32)

    vec1 = jnp.stack([norm1_gain, norm1_shift, out_bias]).astype(F32)
    vec2 = jnp.stack([norm2_gain, norm2_shift, fc2_bias]).astype(F32)
    bias = jnp.concatenate([query_bias, jnp.zeros_like(query_bias), value_bias]).astype(F32)[None]

    kept = []
    chain = None
    for k in range(per):
        pieces = bring(tokens, k)
        shapes = [
            jax.ShapeDtypeStruct((per, rows, width), F32),
            jax.ShapeDtypeStruct((per, rows, width), BF16),
            jax.ShapeDtypeStruct((per, rows, width), BF16),
            jax.ShapeDtypeStruct((per, rows, width), BF16),
            jax.ShapeDtypeStruct((keys, 3 * width), BF16),
            jax.ShapeDtypeStruct((HEADS, rows, keys), BF16),
        ]
        args = [scal[k], *pieces, mask_row[k][None], vec1, bias, qkv_weight, out_weight]
        specs = [SMEM] + [whole(a.shape) for a in args[1:]]
        aliases = {}
        if chain is not None:
            aliases = {len(args) + i: i for i in range(4)}
            args += chain
            specs += [HBM] * 4
        got = pl.pallas_call(
            functools.partial(attention_forward, lay, chain is not None),
            grid=(1,),
            in_specs=specs,
            out_specs=[at_image(k, s.shape) for s in shapes[:4]] + [whole(s.shape) for s in shapes[4:]],
            out_shape=shapes,
            scratch_shapes=[
                pltpu.VMEM((n_seq, slots, width), BF16),
                pltpu.VMEM((rows, width), F32),
            ],
            input_output_aliases=aliases,
            compiler_params=params(1),
            cost_estimate=pl.CostEstimate(
                flops=int(8e9), bytes_accessed=int(12e6), transcendentals=HEADS * rows * keys
            ),
        )(*args)
        chain = list(got[:4])
        kept.append(got[4:])
    hidden, x_all, normed_all, mixed_all = chain

    cot = []
    for j in range(n_seq):
        mine = jnp.concatenate([rows_of(out_cotangent, rank ^ j, k) for k in range(per)], 0)
        cot.append(mine if j == 0 else swap(mine, j))
    steps = hidden_width // CHUNK
    all_rows = per * rows
    shapes = [
        jax.ShapeDtypeStruct((per, n_seq, lay.piece, width), BF16),
        jax.ShapeDtypeStruct((per, rows, width), F32),
        jax.ShapeDtypeStruct((per, rows, width), BF16),
        jax.ShapeDtypeStruct((hidden_width, width), BF16),
        jax.ShapeDtypeStruct((width, hidden_width), BF16),
        jax.ShapeDtypeStruct((1, hidden_width), F32),
        jax.ShapeDtypeStruct((8, width), F32),
    ]
    out_pieces, grad_hidden, grad_att, dw1, dw2, db1, dvec2 = pl.pallas_call(
        functools.partial(feed_forward, lay, per, steps),
        grid=(steps,),
        in_specs=[
            SMEM,
            whole((per, rows, width)),
            *[whole((per, slots, width))] * n_seq,
            pl.BlockSpec((width, CHUNK), lambda i: (0, i)),
            pl.BlockSpec((1, CHUNK), lambda i: (0, i)),
            pl.BlockSpec((CHUNK, width), lambda i: (i, 0)),
            whole(vec2.shape),
        ],
        out_specs=[
            whole(shapes[0].shape),
            whole(shapes[1].shape),
            whole(shapes[2].shape),
            pl.BlockSpec((CHUNK, width), lambda i: (i, 0)),
            pl.BlockSpec((width, CHUNK), lambda i: (0, i)),
            pl.BlockSpec((1, CHUNK), lambda i: (0, i)),
            whole((8, width)),
        ],
        out_shape=shapes,
        scratch_shapes=[
            pltpu.VMEM((n_seq, slots, width), BF16),
            pltpu.VMEM((all_rows, width), F32),
            pltpu.VMEM((all_rows, width), BF16),
            pltpu.VMEM((all_rows, width), BF16),
            pltpu.VMEM((width, all_rows), BF16),
            pltpu.VMEM((all_rows + lay.spare, width), F32),
            pltpu.VMEM((all_rows, width), F32),
            pltpu.VMEM((all_rows, CHUNK), BF16),
            pltpu.VMEM((all_rows, CHUNK), BF16),
        ],
        compiler_params=params(1),
        cost_estimate=pl.CostEstimate(
            flops=12 * all_rows * width * hidden_width,
            bytes_accessed=int(30e6),
            transcendentals=2 * all_rows * hidden_width,
        ),
    )(scal.reshape(-1), hidden, *cot, fc1_weight, fc1_bias.astype(F32)[None], fc2_weight, vec2)

    ex = Exchange(n_dp, n_seq)

    def by_device(array):
        return array.reshape(n_dp, n_seq, array.shape[0] // (n_dp * n_seq), *array.shape[1:])

    fc2_sum = ex.scatter_sum(by_device(dw2), "xyz")
    fc1_sum = ex.scatter_sum(by_device(dw1), "yxz")
    dwo = weight_sum(grad_att.reshape(all_rows, width), mixed_all.reshape(all_rows, width), 256)
    out_sum = ex.scatter_sum(by_device(dwo), "zxy")

    chain = None
    grad_pieces = []
    dvec1 = 0.0
    for k in range(per):
        shapes = [
            jax.ShapeDtypeStruct((n_seq, lay.piece, width), BF16),
            jax.ShapeDtypeStruct((per, rows, 3 * width), BF16),
            jax.ShapeDtypeStruct((8, width), F32),
        ]
        args = [scal[k], grad_att, grad_hidden, x_all, *kept[k], vec1, qkv_weight, out_weight]
        specs = [SMEM] + [at_image(k, a.shape) for a in args[1:4]] + [whole(a.shape) for a in args[4:]]
        aliases = {}
        if chain is not None:
            aliases = {len(args): 1}
            args.append(chain)
            specs.append(HBM)
        pieces, chain, dvec = pl.pallas_call(
            functools.partial(attention_backward, lay, chain is not None),
            grid=(1,),
            in_specs=specs,
            out_specs=[whole(shapes[0].shape), at_image(k, shapes[1].shape), whole(shapes[2].shape)],
            out_shape=shapes,
            scratch_shapes=[
                pltpu.VMEM((rows, width), BF16),
                pltpu.VMEM((rows + lay.spare, width), F32),
            ],
            input_output_aliases=aliases,
            compiler_params=params(1),
            cost_estimate=pl.CostEstimate(
                flops=int(10e9), bytes_accessed=int(15e6), transcendentals=0
            ),
        )(*args)
        grad_pieces.append(pieces)
        dvec1 = dvec1 + dvec
    gp_all = chain.reshape(all_rows, 3 * width)
    dwqkv = weight_sum(gp_all, normed_all.reshape(all_rows, width), 256)
    third = by_device(dwqkv)
    cut = third.shape[2] // 3
    qkv_sum = jnp.concatenate(
        [
            ex.scatter_sum(third[:, :, i * cut : (i + 1) * cut], kind)
            for i, kind in enumerate(("xyz", "yzx", "zxy"))
        ],
        0,
    )

    vectors = [dvec1[0], dvec1[1], dvec1[2], dvec1[3], dvec2[2], dvec2[0], dvec2[1], dvec2[3], db1[0]]
    part = width // (n_dp * n_seq)
    small = jnp.concatenate([by_device(v) for v in vectors], -1)
    small_sum = ex.scatter_sum(small, "xyz")
    small_out = [small_sum[i * part : (i + 1) * part] for i in range(8)] + [small_sum[8 * part :]]

    live = jnp.arange(slots)[None, :] < (
        jnp.sum(jnp.where(jnp.arange(n_seq)[None, :] == rank, row_split, 0), 1) * GRID
    )[:, None]
    live = live[..., None]

    def home(pieces, passed):
        got = [[p[0] if j == 0 else swap(p[j], j) for j in range(n_seq)] for p in pieces]
        parts = []
        for owner in range(n_seq):
            for k in range(per):
                if owner * per + k < images:
                    parts.append(lax.select_n(rank ^ owner, *[got[k][j] for j in range(n_seq)])[:slots])
        return jnp.where(live, jnp.stack(parts), passed)

    output = home([out_pieces[k] for k in range(per)], tokens)
    input_grad = home(grad_pieces, out_cotangent)
    return (
        output,
        input_grad,
        small_out[0],
        small_out[1],
        qkv_sum.T,
        small_out[2],
        small_out[3],
        out_sum.T,
        small_out[4],
        small_out[5],
        small_out[6],
        fc1_sum.T,
        small_out[8],
        fc2_sum.T,
        small_out[7],
    )


def solution(mesh):
    rows = P("dp", "seq", None)
    split = P(("dp", "seq"))
    columns = P(None, ("dp", "seq"))
    return jax.shard_map(
        per_device,
        mesh=mesh,
        in_specs=(rows, P("dp", None), P("dp", None), P("dp")) + (P(),) * 13 + (rows,),
        out_specs=(
            rows,
            rows,
            split,
            split,
            columns,
            split,
            split,
            columns,
            split,
            split,
            split,
            columns,
            split,
            columns,
            split,
        ),
        check_vma=False,
    )
```

time: 1230 us -> 370 us (0.30)
  waiting for transfers between devices: 786 us -> 90.5 us
  matrix products: 179 us -> 0 us
  Pallas kernels: 0 us -> 142 us
  other arithmetic: 98.6 us -> 25.6 us
  starting transfers between devices: 0.5 us -> 54 us
  local copies, waits for them, and re-layouts: 99.9 us -> 50.9 us
  blocking collectives: 41 us -> 0 us
  between operations: 15.5 us -> 2.36 us
    reduce_scatter x4 -> x0, waiting for transfers between devices: 445 us -> none  [the longest x1 142 us: per_device(): lax.psum_scatter(fc1_grad, ('dp', 'seq'), scatter_dimension=1, tiled=True)]
    unnamed x9 -> x0, waiting for transfers between devices: 235 us -> none
    dot_general x18 -> x0, matrix products: 179 us -> none  [the longest x1 18.1 us: per_device(): jnp.einsum('isd,fd->isf', grad_reduced, fc2_weight, preferred_element_typ...]
    pallas_call x0 -> x9, Pallas kernels: none -> 142 us  [the longest x1 49.9 us: per_device(): pl.pallas_call(functools.partial(feed_forward, lay, per, steps), grid=(st...]
    all_gather x1 -> x0, waiting for transfers between devices: 107 us -> none  [per_device(): lax.all_gather(key_values, 'seq', axis=1, tiled=True)]
    ppermute x0 -> x65, waiting for transfers between devices: none -> 90.5 us  [the longest x35 71.8 us: scatter_sum(): got = lax.ppermute(other, axis, [(i, i ^ mask) for i in range(size)])]
    convert_element_type x14 -> x31, other arithmetic: 62.7 us -> 5.86 us  [the longest x24 3.94 us: scatter_sum(): held = held.astype(terms.dtype)]
    ppermute x0 -> x65, starting transfers between devices: none -> 54 us  [the longest x35 31.3 us: scatter_sum(): got = lax.ppermute(other, axis, [(i, i ^ mask) for i in range(size)])]
  transfers between devices with their start and end apart: 7 -> 65, of which waited for: 7 -> 26; matrix products, arithmetic and copies ran while one was open for 9% -> 11% of each run, Pallas kernels for 0% -> 11%
where the time goes in v1:
time: 370 us; the launch traced here: 366 us
  Pallas kernels  142 us (38%)
  waiting for transfers between devices  90.5 us (24%)
  starting transfers between devices  54 us (15%)
  local copies, waits for them, and re-layouts  50.9 us (14%)
  other arithmetic  25.6 us (7%)
    ppermute x35, waiting for transfers between devices, scatter_sum(): got = lax.ppermute(other, axis, [(i, i ^ mask) for i in range(size)])  71.8 us
    pallas_call x1, Pallas kernels, per_device(): pl.pallas_call(functools.partial(feed_forward, lay, per, steps), grid=(st...  49.9 us
    pallas_call x3, Pallas kernels, per_device(): pl.pallas_call(functools.partial(attention_backward, lay, chain is not No...  41.1 us
    pallas_call x3, Pallas kernels, per_device(): pl.pallas_call(functools.partial(attention_forward, lay, chain is not Non...  36.4 us
    ppermute x35, starting transfers between devices, scatter_sum(): got = lax.ppermute(other, axis, [(i, i ^ mask) for i in range(size)])  31.3 us
    ppermute x30, starting transfers between devices, swap(): return lax.ppermute(value, 'seq', [(i, i ^ j) for i in range(n_seq)])  22.7 us
    ppermute x30, waiting for transfers between devices, swap(): return lax.ppermute(value, 'seq', [(i, i ^ j) for i in range(n_seq)])  18.7 us
    pallas_call x2, Pallas kernels, weight_sum(): pl.pallas_call(outer_sum, grid=(n // block,), in_specs=[pl.BlockSpec((row...  15.1 us
  transfers between devices with their start and end apart: 65, of which 26 were waited for; matrix products, arithmetic and copies ran while one was open for 11% of the time, Pallas kernels for 11%

profile of v1, /device:TPU:0, one launch (start us, length us, event | category | flops | bytes accessed | tf_op | source)
XLA Modules:
  0.0 365.9 jit_solution(13829448384010032462)
XLA Ops:
  0.8 2.5 constant_dynamic-slice_fusion.32
  3.8 2.6 collective-permute-start.7
  6.6 1.9 collective-permute-start.4
  17.2 1.9 collective-permute-start.1
  19.1 12.4 %shard_map.289 = (f32[3,336,768]{2,1,0:T(8,128)}, bf16[3,336,768]{2,1,0:T(8,128)(2,1)}, bf16[3,336,768]{2,1,0:T(8,128)(2,1)}, bf16[3,336,768]{2,1,0:T(8,128)(2,1...) custom-call(s32[5]{0:T(128)} %get-tuple-element.179.scal_ref, bf16[1,90,768]{2,1,0:T(8,128)(2,1)} %get-tuple-element.129.p0, ...), custom_call_target="tpu_custom_call" | custom-call | flops 8000000000 | bytes 12000000 | tf_op jit(solution)/shard_map/pallas_call | solution.py:476
  33.6 12.0 %shard_map.290 = (f32[3,336,768]{2,1,0:T(8,128)}, bf16[3,336,768]{2,1,0:T(8,128)(2,1)}, bf16[3,336,768]{2,1,0:T(8,128)(2,1)}, bf16[3,336,768]{2,1,0:T(8,128)(2,1...) custom-call(s32[5]{0:T(128)} %get-tuple-element.180.scal_ref, ...), custom_call_target="tpu_custom_call", output_to_operand_aliasing={{0}: (10, {}), {1}: (11, {}), {2}: (12, {}), {3}: (13, {})} | custom-call | flops 8000000000 | bytes 12000000 | tf_op jit(solution)/shard_map/pallas_call | solution.py:476
  46.9 12.0 %shard_map.291 = (f32[3,336,768]{2,1,0:T(8,128)}, bf16[3,336,768]{2,1,0:T(8,128)(2,1)}, bf16[3,336,768]{2,1,0:T(8,128)(2,1)}, bf16[3,336,768]{2,1,0:T(8,128)(2,1...) custom-call(s32[5]{0:T(128)} %get-tuple-element.181.scal_ref, ...), custom_call_target="tpu_custom_call", output_to_operand_aliasing={{0}: (10, {}), {1}: (11, {}), {2}: (12, {}), {3}: (13, {})} | custom-call | flops 8000000000 | bytes 12000000 | tf_op jit(solution)/shard_map/pallas_call | solution.py:476
  60.0 49.9 %shard_map.292 = (bf16[3,4,96,768]{3,2,1,0:T(8,128)(2,1)}, f32[3,336,768]{2,1,0:T(8,128)}, bf16[3,336,768]{2,1,0:T(8,128)(2,1)}, bf16[3072,768]{1,0:T(8,128)(2,1...) custom-call(s32[15]{0:T(128)} %reshape.312.scal_ref, ...), custom_call_target="tpu_custom_call" | custom-call | flops 28538044416 | bytes 30000000 | tf_op jit(solution)/shard_map/pallas_call | solution.py:511
  109.8 13.8 %shard_map.293 = (bf16[4,96,768]{2,1,0:T(8,128)(2,1)}, bf16[3,336,2304]{2,1,0:T(8,128)(2,1)}, f32[8,768]{1,0:T(8,128)}) custom-call(s32[5]{0:T(128)} %get-tuple-element.179.scal_ref, bf16[3,336,768]{2,1,0:T(8,128)(2,1)} %get-tuple-element.59.ga_ref, f32[3,336,768]{2,1,0:T(8,128)} %get-tuple-element.60.gh_ref, bf16[3,336,768]{2,1,0:T(8,128)(2,1)} %get-tuple-element.61.x_ref, ...), custom_call_target="tpu_custom_call" | custom-call | flops 10000000000 | bytes 15000000 | tf_op jit(solution)/shard_map/pallas_call | solution.py:578
  123.6 13.6 %shard_map.294 = (bf16[4,96,768]{2,1,0:T(8,128)(2,1)}, bf16[3,336,2304]{2,1,0:T(8,128)(2,1)}, f32[8,768]{1,0:T(8,128)}) custom-call(s32[5]{0:T(128)} %get-tuple-element.180.scal_ref, bf16[3,336,768]{2,1,0:T(8,128)(2,1)} %get-tuple-element.59.ga_ref, f32[3,336,768]{2,1,0:T(8,128)} %get-tuple-element.60.gh_ref, ...), custom_call_target="tpu_custom_call", output_to_operand_aliasing={{1}: (9, {})} | custom-call | flops 10000000000 | bytes 15000000 | tf_op jit(solution)/shard_map/pallas_call | solution.py:578
  137.2 13.6 %shard_map.295 = (bf16[4,96,768]{2,1,0:T(8,128)(2,1)}, bf16[3,336,2304]{2,1,0:T(8,128)(2,1)}, f32[8,768]{1,0:T(8,128)}) custom-call(s32[5]{0:T(128)} %get-tuple-element.181.scal_ref, bf16[3,336,768]{2,1,0:T(8,128)(2,1)} %get-tuple-element.59.ga_ref, f32[3,336,768]{2,1,0:T(8,128)} %get-tuple-element.60.gh_ref, ...), custom_call_target="tpu_custom_call", output_to_operand_aliasing={{1}: (9, {})} | custom-call | flops 10000000000 | bytes 15000000 | tf_op jit(solution)/shard_map/pallas_call | solution.py:578
  150.9 10.2 %shard_map.296 = bf16[2304,768]{1,0:T(8,128)(2,1)} custom-call(bf16[1008,2304]{1,0:T(8,128)(2,1)} %bitcast.339, bf16[1008,768]{1,0:T(8,128)(2,1)} %bitcast.341), custom_call_target="tpu_custom_call" | custom-call | flops 3567255552 | bytes 9732096 | tf_op jit(solution)/shard_map/pallas_call | solution.py:322
  161.1 3.2 fusion.42
  164.3 4.3 %constant_dynamic-slice_fusion.1 = (bf16[2,2,2,2,1,24,3072]{6,5,4,3,2,1,0:T(8,128)(2,1)S(1)}, bf16[2,2,2,2,1,24,3072]{6,5,4,3,2,1,0:T(8,128)(2,1)}) fusion(bf16[2,2,2,2,2,24,3072]{6,5,4,3,2,1,0:T(8,128)(2,1)} %bitcast.323, s32[]{:T(128)S(6)} %select_n.807, s32[]{:T(128)S(6)} %select_n.808), kind=kLoop, calls=%fused_computation.151 | loop fusion | bytes 9437192 | tf_op jit(solution)/shard_map/jit(dynamic_index_in_dim)/dynamic_slice | solution.py:383
  176.0 1.5 slice_reduce_fusion.4
  183.6 2.0 reduce.23
  186.9 1.7 concatenate.75
  189.7 2.7 slice_bitcast_fusion.15
  195.7 5.0 %constant_dynamic-slice_fusion.3 = (bf16[2,2,2,2,1,96,768]{6,5,4,3,2,1,0:T(8,128)(2,1)}, bf16[2,2,2,2,1,96,768]{6,5,4,3,2,1,0:T(8,128)(2,1)}) fusion(bf16[2,2,2,2,2,96,768]{6,5,4,3,2,1,0:T(8,128)(2,1)} %bitcast.322, s32[]{:T(128)S(6)} %select_n.807, s32[]{:T(128)S(6)} %select_n.808), kind=kLoop, calls=%fused_computation.153 | loop fusion | bytes 9437192 | tf_op jit(solution)/shard_map/jit(dynamic_index_in_dim)/dynamic_slice | solution.py:383
  200.8 1.6 collective-permute-start.31
  202.3 4.9 %shard_map.297 = bf16[768,768]{1,0:T(8,128)(2,1)} custom-call(bf16[1008,768]{1,0:T(8,128)(2,1)} %bitcast.340, bf16[1008,768]{1,0:T(8,128)(2,1)} %bitcast.342), custom_call_target="tpu_custom_call" | custom-call | flops 1189085184 | bytes 4276224 | tf_op jit(solution)/shard_map/pallas_call | solution.py:322
  208.4 1.6 constant_dynamic-slice_fusion.5
  211.1 1.6 collective-permute-start.33
  213.0 1.5 copy-done.2
  216.5 2.6 collective-permute-start.34
  219.2 1.8 collective-permute-done.34
  227.3 2.8 collective-permute-done.22
  230.1 2.2 collective-permute-done.23
  238.6 3.6 collective-permute-done.25
  243.2 2.4 collective-permute-done.26
  246.8 1.9 collective-permute-done.29
  249.2 2.5 collective-permute-done.19
  251.8 3.1 collective-permute-done.20
  263.7 2.1 broadcast_select_fusion
  269.2 6.3 %collective-permute-done.51 = bf16[2,2,2,24,768]{4,3,2,0,1:T(8,128)(2,1)S(1)} collective-permute-done((bf16[2,2,2,24,768]{4,3,2,0,1:T(8,128)(2,1)S(1)}, bf16[2,2,2,24,768]{4,3,2,0,1:T(8,128)(2,1)S(1)}, u32[]{:S(2)}, u32[]{:S(2)}) %collective-permute-start.51) | collective-permute-done | bytes 294944 | tf_op jit(solution)/shard_map/ppermute | solution.py:384
  278.3 5.3 %collective-permute-done.46 = bf16[2,2,2,24,768]{4,3,2,0,1:T(8,128)(2,1)S(1)} collective-permute-done((bf16[2,2,2,24,768]{4,3,2,0,1:T(8,128)(2,1)S(1)}, bf16[2,2,2,24,768]{4,3,2,0,1:T(8,128)(2,1)S(1)}, u32[]{:S(2)}, u32[]{:S(2)}) %collective-permute-start.46) | collective-permute-done | bytes 294944 | tf_op jit(solution)/shard_map/ppermute | solution.py:384
  284.8 2.7 collective-permute-start.53
  289.0 1.6 collective-permute-start.38
  290.6 2.9 collective-permute-start.43
  294.9 2.2 collective-permute-done.43
  297.1 1.6 collective-permute-start.39
  307.6 19.2 %collective-permute-done.61 = bf16[2,2,2,24,3072]{4,3,0,1,2:T(8,128)(2,1)S(1)} collective-permute-done((bf16[2,2,2,24,3072]{4,3,0,1,2:T(8,128)(2,1)S(1)}, bf16[2,2,2,24,3072]{4,3,0,1,2:T(8,128)(2,1)S(1)}, u32[]{:S(2)}, u32[]{:S(2)}) %collective-permute-start.61) | collective-permute-done | bytes 1179680 | tf_op jit(solution)/shard_map/ppermute | solution.py:384
  329.0 5.6 %collective-permute-done.56 = bf16[2,2,2,96,768]{4,3,0,1,2:T(8,128)(2,1)S(1)} collective-permute-done((bf16[2,2,2,96,768]{4,3,0,1,2:T(8,128)(2,1)S(1)}, bf16[2,2,2,96,768]{4,3,0,1,2:T(8,128)(2,1)S(1)}, u32[]{:S(2)}, u32[]{:S(2)}) %collective-permute-start.56) | collective-permute-done | bytes 1179680 | tf_op jit(solution)/shard_map/ppermute | solution.py:384
  335.0 7.6 %collective-permute-done.62 = bf16[2,2,24,3072]{3,2,0,1:T(8,128)(2,1)S(1)} collective-permute-done((bf16[2,2,24,3072]{3,2,0,1:T(8,128)(2,1)S(1)}, bf16[2,2,24,3072]{3,2,0,1:T(8,128)(2,1)S(1)}, u32[]{:S(2)}, u32[]{:S(2)}) %collective-permute-start.62) | collective-permute-done | bytes 589856 | tf_op jit(solution)/shard_map/ppermute | solution.py:384
  345.7 6.2 %collective-permute-done.63 = bf16[2,24,3072]{2,1,0:T(8,128)(2,1)S(1)} collective-permute-done((bf16[2,24,3072]{2,1,0:T(8,128)(2,1)S(1)}, bf16[2,24,3072]{2,1,0:T(8,128)(2,1)S(1)}, u32[]{:S(2)}, u32[]{:S(2)}) %collective-permute-start.63) | collective-permute-done | bytes 294944 | tf_op jit(solution)/shard_map/ppermute | solution.py:384
  352.7 5.0 %collective-permute-done.58 = bf16[2,96,768]{2,1,0:T(8,128)(2,1)S(1)} collective-permute-done((bf16[2,96,768]{2,1,0:T(8,128)(2,1)S(1)}, bf16[2,96,768]{2,1,0:T(8,128)(2,1)S(1)}, u32[]{:S(2)}, u32[]{:S(2)}) %collective-permute-start.58) | collective-permute-done | bytes 294944 | tf_op jit(solution)/shard_map/ppermute | solution.py:384
  357.9 1.9 collective-permute-done.64
  360.6 4.4 %collective-permute-done.59 = bf16[96,768]{1,0:T(8,128)(2,1)S(1)} collective-permute-done((bf16[96,768]{1,0:T(8,128)(2,1)S(1)}, bf16[96,768]{1,0:T(8,128)(2,1)S(1)}, u32[]{:S(2)}, u32[]{:S(2)}) %collective-permute-start.59) | collective-permute-done | bytes 147488 | tf_op jit(solution)/shard_map/ppermute | solution.py:384
  (368 shorter events, 88.0 us)
Async XLA Ops:
  3.3 13.6 %collective-permute-start.6 = (bf16[1,90,768]{2,1,0:T(8,128)(2,1)S(1)}, bf16[1,90,768]{2,1,0:T(8,128)(2,1)}, u32[]{:S(2)}, u32[]{:S(2)}) collective-permute-start(bf16[1,90,768]{2,1,0:T(8,128)(2,1)S(1)} %get-tuple-element.128), channel_id=1, source_target_pairs={{0,1},{1,0},{2,3},{3,2},{4,5},{5,4},{6,7},{7,6},{8,9},{9,8},{10,11... | collective-permute-start | bytes 414728 | tf_op jit(solution)/shard_map/ppermute | solution.py:422
  3.8 13.1 %collective-permute-start.7 = (bf16[1,90,768]{2,1,0:T(8,128)(2,1)S(1)}, bf16[1,90,768]{2,1,0:T(8,128)(2,1)}, u32[]{:S(2)}, u32[]{:S(2)}) collective-permute-start(bf16[1,90,768]{2,1,0:T(8,128)(2,1)S(1)} %get-tuple-element.127), channel_id=1, source_target_pairs={{0,2},{1,3},{2,0},{3,1},{4,6},{5,7},{6,4},{7,5},{8,10},{9,11},{10,... | collective-permute-start | bytes 414728 | tf_op jit(solution)/shard_map/ppermute | solution.py:422
  6.4 10.8 %collective-permute-start.8 = (bf16[1,90,768]{2,1,0:T(8,128)(2,1)S(1)}, bf16[1,90,768]{2,1,0:T(8,128)(2,1)}, u32[]{:S(2)}, u32[]{:S(2)}) collective-permute-start(bf16[1,90,768]{2,1,0:T(8,128)(2,1)S(1)} %get-tuple-element.126), channel_id=1, source_target_pairs={{0,3},{1,2},{2,1},{3,0},{4,7},{5,6},{6,5},{7,4},{8,11},{9,10},{10,... | collective-permute-start | bytes 414728 | tf_op jit(solution)/shard_map/ppermute | solution.py:422
  6.4 25.0 %collective-permute-start.3 = (bf16[1,90,768]{2,1,0:T(8,128)(2,1)S(1)}, bf16[1,90,768]{2,1,0:T(8,128)(2,1)S(1)}, u32[]{:S(2)}, u32[]{:S(2)}) collective-permute-start(bf16[1,90,768]{2,1,0:T(8,128)(2,1)S(1)} %get-tuple-element.132), channel_id=1, source_target_pairs={{0,1},{1,0},{2,3},{3,2},{4,5},{5,4},{6,7},{7,6},{8,9},{9,8},{10,11... | collective-permute-start | bytes 414728 | tf_op jit(solution)/shard_map/ppermute | solution.py:422
  6.6 25.0 %collective-permute-start.4 = (bf16[1,90,768]{2,1,0:T(8,128)(2,1)S(1)}, bf16[1,90,768]{2,1,0:T(8,128)(2,1)}, u32[]{:S(2)}, u32[]{:S(2)}) collective-permute-start(bf16[1,90,768]{2,1,0:T(8,128)(2,1)S(1)} %get-tuple-element.131), channel_id=1, source_target_pairs={{0,2},{1,3},{2,0},{3,1},{4,6},{5,7},{6,4},{7,5},{8,10},{9,11},{10,... | collective-permute-start | bytes 414728 | tf_op jit(solution)/shard_map/ppermute | solution.py:422
  16.9 16.1 %collective-permute-start.5 = (bf16[1,90,768]{2,1,0:T(8,128)(2,1)S(1)}, bf16[1,90,768]{2,1,0:T(8,128)(2,1)S(1)}, u32[]{:S(2)}, u32[]{:S(2)}) collective-permute-start(bf16[1,90,768]{2,1,0:T(8,128)(2,1)S(1)} %get-tuple-element.130), channel_id=1, source_target_pairs={{0,3},{1,2},{2,1},{3,0},{4,7},{5,6},{6,5},{7,4},{8,11},{9,10},{10,... | collective-permute-start | bytes 414728 | tf_op jit(solution)/shard_map/ppermute | solution.py:422
  16.9 28.7 %collective-permute-start = (bf16[1,90,768]{2,1,0:T(8,128)(2,1)S(1)}, bf16[1,90,768]{2,1,0:T(8,128)(2,1)S(1)}, u32[]{:S(2)}, u32[]{:S(2)}) collective-permute-start(bf16[1,90,768]{2,1,0:T(8,128)(2,1)S(1)} %get-tuple-element.136), channel_id=1, source_target_pairs={{0,1},{1,0},{2,3},{3,2},{4,5},{5,4},{6,7},{7,6},{8,9},{9,8},{10,11... | collective-permute-start | bytes 414728 | tf_op jit(solution)/shard_map/ppermute | solution.py:422
  17.2 29.0 %collective-permute-start.1 = (bf16[1,90,768]{2,1,0:T(8,128)(2,1)S(1)}, bf16[1,90,768]{2,1,0:T(8,128)(2,1)S(1)}, u32[]{:S(2)}, u32[]{:S(2)}) collective-permute-start(bf16[1,90,768]{2,1,0:T(8,128)(2,1)S(1)} %get-tuple-element.135), channel_id=1, source_target_pairs={{0,2},{1,3},{2,0},{3,1},{4,6},{5,7},{6,4},{7,5},{8,10},{9,11},{10,... | collective-permute-start | bytes 414728 | tf_op jit(solution)/shard_map/ppermute | solution.py:422
  31.5 14.6 %collective-permute-start.2 = (bf16[1,90,768]{2,1,0:T(8,128)(2,1)S(1)}, bf16[1,90,768]{2,1,0:T(8,128)(2,1)S(1)}, u32[]{:S(2)}, u32[]{:S(2)}) collective-permute-start(bf16[1,90,768]{2,1,0:T(8,128)(2,1)S(1)} %get-tuple-element.134), channel_id=1, source_target_pairs={{0,3},{1,2},{2,1},{3,0},{4,7},{5,6},{6,5},{7,4},{8,11},{9,10},{10,... | collective-permute-start | bytes 414728 | tf_op jit(solution)/shard_map/ppermute | solution.py:422
  31.6 27.3 %collective-permute-start.10 = (bf16[3,90,768]{2,1,0:T(8,128)(2,1)S(1)}, bf16[3,90,768]{2,1,0:T(8,128)(2,1)S(1)}, u32[]{:S(2)}, u32[]{:S(2)}) collective-permute-start(bf16[3,90,768]{2,1,0:T(8,128)(2,1)S(1)} %pad_maximum_fusion.2), channel_id=1, source_target_pairs={{0,2},{1,3},{2,0},{3,1},{4,6},{5,7},{6,4},{7,5},{8,10},{9,11},{10,... | collective-permute-start | bytes 1244168 | tf_op jit(solution)/shard_map/ppermute | solution.py:422
  33.0 25.9 %collective-permute-start.11 = (bf16[3,90,768]{2,1,0:T(8,128)(2,1)S(1)}, bf16[3,90,768]{2,1,0:T(8,128)(2,1)S(1)}, u32[]{:S(2)}, u32[]{:S(2)}) collective-permute-start(bf16[3,90,768]{2,1,0:T(8,128)(2,1)S(1)} %pad_maximum_fusion.3), channel_id=1, source_target_pairs={{0,3},{1,2},{2,1},{3,0},{4,7},{5,6},{6,5},{7,4},{8,11},{9,10},{10,... | collective-permute-start | bytes 1244168 | tf_op jit(solution)/shard_map/ppermute | solution.py:422
  45.6 13.3 %collective-permute-start.9 = (bf16[3,90,768]{2,1,0:T(8,128)(2,1)S(1)}, bf16[3,90,768]{2,1,0:T(8,128)(2,1)S(1)}, u32[]{:S(2)}, u32[]{:S(2)}) collective-permute-start(bf16[3,90,768]{2,1,0:T(8,128)(2,1)S(1)} %pad_maximum_fusion.1), channel_id=1, source_target_pairs={{0,1},{1,0},{2,3},{3,2},{4,5},{5,4},{6,7},{7,6},{8,9},{9,8},{10,11... | collective-permute-start | bytes 1244168 | tf_op jit(solution)/shard_map/ppermute | solution.py:422
  189.6 11.2 %collective-permute-start.30 = (f32[2,2,2,2,288]{4,3,2,1,0:T(2,128)S(1)}, f32[2,2,2,2,288]{4,3,2,1,0:T(2,128)S(1)}, u32[]{:S(2)}, u32[]{:S(2)}) collective-permute-start(f32[2,2,2,2,288]{4,3,2,1,0:T(2,128)S(1)} %bitcast.331), channel_id=1, source_target_pairs={{0,1},{1,0},{2,3},{3,2},{4,5},{5,4},{6,7},{7,6},{8,9},{9,8},{10,11... | collective-permute-start | bytes 55304 | tf_op jit(solution)/shard_map/ppermute | solution.py:384
  192.4 30.9 %collective-permute-start.12 = (bf16[96,768]{1,0:T(8,128)(2,1)}, bf16[96,768]{1,0:T(8,128)(2,1)}, u32[]{:S(2)}, u32[]{:S(2)}) collective-permute-start(bf16[96,768]{1,0:T(8,128)(2,1)} %get-tuple-element.112), channel_id=1, source_target_pairs={{0,1},{1,0},{2,3},{3,2},{4,5},{5,4},{6,7},{7,6},{8,9},{9,8},{10,11... | collective-permute-start | bytes 442376 | tf_op jit(solution)/shard_map/ppermute | solution.py:422
  192.9 31.5 %collective-permute-start.14 = (bf16[96,768]{1,0:T(8,128)(2,1)}, bf16[96,768]{1,0:T(8,128)(2,1)}, u32[]{:S(2)}, u32[]{:S(2)}) collective-permute-start(bf16[96,768]{1,0:T(8,128)(2,1)} %get-tuple-element.110), channel_id=1, source_target_pairs={{0,3},{1,2},{2,1},{3,0},{4,7},{5,6},{6,5},{7,4},{8,11},{9,10},{10,... | collective-permute-start | bytes 442376 | tf_op jit(solution)/shard_map/ppermute | solution.py:422
  194.0 39.4 %collective-permute-start.15 = (bf16[96,768]{1,0:T(8,128)(2,1)}, bf16[96,768]{1,0:T(8,128)(2,1)}, u32[]{:S(2)}, u32[]{:S(2)}) collective-permute-start(bf16[96,768]{1,0:T(8,128)(2,1)} %get-tuple-element.108), channel_id=1, source_target_pairs={{0,1},{1,0},{2,3},{3,2},{4,5},{5,4},{6,7},{7,6},{8,9},{9,8},{10,11... | collective-permute-start | bytes 442376 | tf_op jit(solution)/shard_map/ppermute | solution.py:422
  215.5 7.9 %collective-permute-start.13 = (bf16[96,768]{1,0:T(8,128)(2,1)S(1)}, bf16[96,768]{1,0:T(8,128)(2,1)S(1)}, u32[]{:S(2)}, u32[]{:S(2)}) collective-permute-start(bf16[96,768]{1,0:T(8,128)(2,1)S(1)} %copy-done.25), channel_id=1, source_target_pairs={{0,2},{1,3},{2,0},{3,1},{4,6},{5,7},{6,4},{7,5},{8,10},{9,11},{10,... | collective-permute-start | bytes 442376 | tf_op jit(solution)/shard_map/ppermute | solution.py:422
  221.0 13.2 %collective-permute-start.16 = (bf16[96,768]{1,0:T(8,128)(2,1)S(1)}, bf16[96,768]{1,0:T(8,128)(2,1)S(1)}, u32[]{:S(2)}, u32[]{:S(2)}) collective-permute-start(bf16[96,768]{1,0:T(8,128)(2,1)S(1)} %copy-done.22), channel_id=1, source_target_pairs={{0,2},{1,3},{2,0},{3,1},{4,6},{5,7},{6,4},{7,5},{8,10},{9,11},{10,... | collective-permute-start | bytes 442376 | tf_op jit(solution)/shard_map/ppermute | solution.py:422
  224.4 7.9 %collective-permute-start.23 = (bf16[96,768]{1,0:T(8,128)(2,1)S(1)}, bf16[96,768]{1,0:T(8,128)(2,1)S(1)}, u32[]{:S(2)}, u32[]{:S(2)}) collective-permute-start(bf16[96,768]{1,0:T(8,128)(2,1)S(1)} %get-tuple-element.153), channel_id=1, source_target_pairs={{0,3},{1,2},{2,1},{3,0},{4,7},{5,6},{6,5},{7,4},{8,11},{9,10},{10,... | collective-permute-start | bytes 442376 | tf_op jit(solution)/shard_map/ppermute | solution.py:422
  226.3 9.2 %collective-permute-start.17 = (bf16[96,768]{1,0:T(8,128)(2,1)S(1)}, bf16[96,768]{1,0:T(8,128)(2,1)S(1)}, u32[]{:S(2)}, u32[]{:S(2)}) collective-permute-start(bf16[96,768]{1,0:T(8,128)(2,1)S(1)} %copy-done.20), channel_id=1, source_target_pairs={{0,3},{1,2},{2,1},{3,0},{4,7},{5,6},{6,5},{7,4},{8,11},{9,10},{10,... | collective-permute-start | bytes 442376 | tf_op jit(solution)/shard_map/ppermute | solution.py:422
  230.1 7.2 %collective-permute-start.27 = (bf16[96,768]{1,0:T(8,128)(2,1)S(1)}, bf16[96,768]{1,0:T(8,128)(2,1)S(1)}, u32[]{:S(2)}, u32[]{:S(2)}) collective-permute-start(bf16[96,768]{1,0:T(8,128)(2,1)S(1)} %copy-done.24), channel_id=1, source_target_pairs={{0,1},{1,0},{2,3},{3,2},{4,5},{5,4},{6,7},{7,6},{8,9},{9,8},{10,11... | collective-permute-start | bytes 442376 | tf_op jit(solution)/shard_map/ppermute | solution.py:422
  232.4 13.8 %collective-permute-start.28 = (bf16[96,768]{1,0:T(8,128)(2,1)S(1)}, bf16[96,768]{1,0:T(8,128)(2,1)S(1)}, u32[]{:S(2)}, u32[]{:S(2)}) collective-permute-start(bf16[96,768]{1,0:T(8,128)(2,1)S(1)} %copy-done.18), channel_id=1, source_target_pairs={{0,2},{1,3},{2,0},{3,1},{4,6},{5,7},{6,4},{7,5},{8,10},{9,11},{10,... | collective-permute-start | bytes 442376 | tf_op jit(solution)/shard_map/ppermute | solution.py:422
  234.3 8.0 %collective-permute-start.25 = (bf16[96,768]{1,0:T(8,128)(2,1)S(1)}, bf16[96,768]{1,0:T(8,128)(2,1)S(1)}, u32[]{:S(2)}, u32[]{:S(2)}) collective-permute-start(bf16[96,768]{1,0:T(8,128)(2,1)S(1)} %copy-done.21), channel_id=1, source_target_pairs={{0,2},{1,3},{2,0},{3,1},{4,6},{5,7},{6,4},{7,5},{8,10},{9,11},{10,... | collective-permute-start | bytes 442376 | tf_op jit(solution)/shard_map/ppermute | solution.py:422
  235.5 10.0 %collective-permute-start.26 = (bf16[96,768]{1,0:T(8,128)(2,1)S(1)}, bf16[96,768]{1,0:T(8,128)(2,1)S(1)}, u32[]{:S(2)}, u32[]{:S(2)}) collective-permute-start(bf16[96,768]{1,0:T(8,128)(2,1)S(1)} %copy-done.19), channel_id=1, source_target_pairs={{0,3},{1,2},{2,1},{3,0},{4,7},{5,6},{6,5},{7,4},{8,11},{9,10},{10,... | collective-permute-start | bytes 442376 | tf_op jit(solution)/shard_map/ppermute | solution.py:422
  237.4 11.3 %collective-permute-start.29 = (bf16[96,768]{1,0:T(8,128)(2,1)S(1)}, bf16[96,768]{1,0:T(8,128)(2,1)S(1)}, u32[]{:S(2)}, u32[]{:S(2)}) collective-permute-start(bf16[96,768]{1,0:T(8,128)(2,1)S(1)} %copy-done.17), channel_id=1, source_target_pairs={{0,3},{1,2},{2,1},{3,0},{4,7},{5,6},{6,5},{7,4},{8,11},{9,10},{10,... | collective-permute-start | bytes 442376 | tf_op jit(solution)/shard_map/ppermute | solution.py:422
  238.3 10.4 %collective-permute-start.18 = (bf16[96,768]{1,0:T(8,128)(2,1)S(1)}, bf16[96,768]{1,0:T(8,128)(2,1)S(1)}, u32[]{:S(2)}, u32[]{:S(2)}) collective-permute-start(bf16[96,768]{1,0:T(8,128)(2,1)S(1)} %copy-done.16), channel_id=1, source_target_pairs={{0,1},{1,0},{2,3},{3,2},{4,5},{5,4},{6,7},{7,6},{8,9},{9,8},{10,11... | collective-permute-start | bytes 442376 | tf_op jit(solution)/shard_map/ppermute | solution.py:422
  242.2 9.5 %collective-permute-start.19 = (bf16[96,768]{1,0:T(8,128)(2,1)S(1)}, bf16[96,768]{1,0:T(8,128)(2,1)S(1)}, u32[]{:S(2)}, u32[]{:S(2)}) collective-permute-start(bf16[96,768]{1,0:T(8,128)(2,1)S(1)} %copy-done.15), channel_id=1, source_target_pairs={{0,2},{1,3},{2,0},{3,1},{4,6},{5,7},{6,4},{7,5},{8,10},{9,11},{10,... | collective-permute-start | bytes 442376 | tf_op jit(solution)/shard_map/ppermute | solution.py:422
  245.5 9.4 %collective-permute-start.20 = (bf16[96,768]{1,0:T(8,128)(2,1)S(1)}, bf16[96,768]{1,0:T(8,128)(2,1)S(1)}, u32[]{:S(2)}, u32[]{:S(2)}) collective-permute-start(bf16[96,768]{1,0:T(8,128)(2,1)S(1)} %copy-done.14), channel_id=1, source_target_pairs={{0,3},{1,2},{2,1},{3,0},{4,7},{5,6},{6,5},{7,4},{8,11},{9,10},{10,... | collective-permute-start | bytes 442376 | tf_op jit(solution)/shard_map/ppermute | solution.py:422
  246.2 54.5 %collective-permute-start.60 = (bf16[2,2,2,2,24,3072]{5,4,0,1,3,2:T(8,128)(2,1)S(1)}, bf16[2,2,2,2,24,3072]{5,4,0,1,3,2:T(8,128)(2,1)S(1)}, u32[]{:S(2)}, u32[]{:S(2)}) collective-permute-start(bf16[2,2,2,2,24,3072]{5,4,0,1,3,2:T(8,128)(2,1)S(1)} %bitcast.326), channel_id=1, source_target_pairs={{0,1},{1,0},{2,3},{3,2},{4,5},{5,4},{6,7},{7,6},{8,9},{9,8},{10,11... | collective-permute-start | bytes 7077896 | tf_op jit(solution)/shard_map/ppermute | solution.py:384
  248.7 57.0 %collective-permute-start.55 = (bf16[2,2,2,2,96,768]{5,4,0,1,2,3:T(8,128)(2,1)S(1)}, bf16[2,2,2,2,96,768]{5,4,0,1,2,3:T(8,128)(2,1)S(1)}, u32[]{:S(2)}, u32[]{:S(2)}) collective-permute-start(bf16[2,2,2,2,96,768]{5,4,0,1,2,3:T(8,128)(2,1)S(1)} %bitcast.325), channel_id=1, source_target_pairs={{0,1},{1,0},{2,3},{3,2},{4,5},{5,4},{6,7},{7,6},{8,9},{9,8},{10,11... | collective-permute-start | bytes 7077896 | tf_op jit(solution)/shard_map/ppermute | solution.py:384
  248.7 17.1 %collective-permute-start.50 = (bf16[2,2,2,2,24,768]{5,4,3,0,2,1:T(8,128)(2,1)S(1)}, bf16[2,2,2,2,24,768]{5,4,3,0,2,1:T(8,128)(2,1)S(1)}, u32[]{:S(2)}, u32[]{:S(2)}) collective-permute-start(bf16[2,2,2,2,24,768]{5,4,3,0,2,1:T(8,128)(2,1)S(1)} %bitcast.330), channel_id=1, source_target_pairs={{0,1},{1,0},{2,3},{3,2},{4,5},{5,4},{6,7},{7,6},{8,9},{9,8},{10,11... | collective-permute-start | bytes 1769480 | tf_op jit(solution)/shard_map/ppermute | solution.py:384
  251.7 14.8 %collective-permute-start.35 = (bf16[2,2,2,2,24,768]{5,4,3,2,1,0:T(8,128)(2,1)S(1)}, bf16[2,2,2,2,24,768]{5,4,3,2,1,0:T(8,128)(2,1)S(1)}, u32[]{:S(2)}, u32[]{:S(2)}) collective-permute-start(bf16[2,2,2,2,24,768]{5,4,3,2,1,0:T(8,128)(2,1)S(1)} %dynamic-slice_bitcast_fusion.4), channel_id=1, source_target_pairs={{0,1},{1,0},{2,3},{3,2},{4,5},{5,4},{6,7},{7,6},{8,9},{9,8},{10,11... | collective-permute-start | bytes 1769480 | tf_op jit(solution)/shard_map/ppermute | solution.py:384
  254.9 12.2 %collective-permute-start.40 = (bf16[2,2,2,2,24,768]{5,4,2,0,1,3:T(8,128)(2,1)S(1)}, bf16[2,2,2,2,24,768]{5,4,2,0,1,3:T(8,128)(2,1)S(1)}, u32[]{:S(2)}, u32[]{:S(2)}) collective-permute-start(bf16[2,2,2,2,24,768]{5,4,2,0,1,3:T(8,128)(2,1)S(1)} %bitcast.328), channel_id=1, source_target_pairs={{0,1},{1,0},{2,3},{3,2},{4,5},{5,4},{6,7},{7,6},{8,9},{9,8},{10,11... | collective-permute-start | bytes 1769480 | tf_op jit(solution)/shard_map/ppermute | solution.py:384
  266.5 9.0 %collective-permute-start.51 = (bf16[2,2,2,24,768]{4,3,2,0,1:T(8,128)(2,1)S(1)}, bf16[2,2,2,24,768]{4,3,2,0,1:T(8,128)(2,1)S(1)}, u32[]{:S(2)}, u32[]{:S(2)}) collective-permute-start(bf16[2,2,2,24,768]{4,3,2,0,1:T(8,128)(2,1)S(1)} %dynamic-slice_bitcast_fusion.7), channel_id=1, source_target_pairs={{0,8},{4,12},{8,0},{12,4},{16,24},{20,28},{24,16},{28,20},{1,9},{5... | collective-permute-start | bytes 884744 | tf_op jit(solution)/shard_map/ppermute | solution.py:384
  267.2 8.9 %collective-permute-start.36 = (bf16[2,2,2,24,768]{4,3,2,1,0:T(8,128)(2,1)S(1)}, bf16[2,2,2,24,768]{4,3,2,1,0:T(8,128)(2,1)S(1)}, u32[]{:S(2)}, u32[]{:S(2)}) collective-permute-start(bf16[2,2,2,24,768]{4,3,2,1,0:T(8,128)(2,1)S(1)} %dynamic-slice_bitcast_fusion.10), channel_id=1, source_target_pairs={{0,4},{4,0},{8,12},{12,8},{16,20},{20,16},{24,28},{28,24},{1,5},{5... | collective-permute-start | bytes 884744 | tf_op jit(solution)/shard_map/ppermute | solution.py:384
  268.0 9.2 %collective-permute-start.41 = (bf16[2,2,2,24,768]{4,3,2,0,1:T(8,128)(2,1)S(1)}, bf16[2,2,2,24,768]{4,3,2,0,1:T(8,128)(2,1)S(1)}, u32[]{:S(2)}, u32[]{:S(2)}) collective-permute-start(bf16[2,2,2,24,768]{4,3,2,0,1:T(8,128)(2,1)S(1)} %dynamic-slice_bitcast_fusion.9), channel_id=1, source_target_pairs={{0,2},{1,3},{2,0},{3,1},{4,6},{5,7},{6,4},{7,5},{8,10},{9,11},{10,... | collective-permute-start | bytes 884744 | tf_op jit(solution)/shard_map/ppermute | solution.py:384
  275.5 8.1 %collective-permute-start.46 = (bf16[2,2,2,24,768]{4,3,2,0,1:T(8,128)(2,1)S(1)}, bf16[2,2,2,24,768]{4,3,2,0,1:T(8,128)(2,1)S(1)}, u32[]{:S(2)}, u32[]{:S(2)}) collective-permute-start(bf16[2,2,2,24,768]{4,3,2,0,1:T(8,128)(2,1)S(1)} %dynamic-slice_bitcast_fusion.8), channel_id=1, source_target_pairs={{0,8},{4,12},{8,0},{12,4},{16,24},{20,28},{24,16},{28,20},{1,9},{5... | collective-permute-start | bytes 884744 | tf_op jit(solution)/shard_map/ppermute | solution.py:384
  276.0 8.1 %collective-permute-start.52 = (bf16[2,2,24,768]{3,2,1,0:T(8,128)(2,1)S(1)}, bf16[2,2,24,768]{3,2,1,0:T(8,128)(2,1)S(1)}, u32[]{:S(2)}, u32[]{:S(2)}) collective-permute-start(bf16[2,2,24,768]{3,2,1,0:T(8,128)(2,1)S(1)} %dynamic-slice_bitcast_fusion.13), channel_id=1, source_target_pairs={{0,4},{4,0},{8,12},{12,8},{16,20},{20,16},{24,28},{28,24},{1,5},{5... | collective-permute-start | bytes 442376 | tf_op jit(solution)/shard_map/ppermute | solution.py:384
  277.2 7.6 %collective-permute-start.37 = (bf16[2,2,24,768]{3,2,1,0:T(8,128)(2,1)S(1)}, bf16[2,2,24,768]{3,2,1,0:T(8,128)(2,1)S(1)}, u32[]{:S(2)}, u32[]{:S(2)}) collective-permute-start(bf16[2,2,24,768]{3,2,1,0:T(8,128)(2,1)S(1)} %dynamic-slice_bitcast_fusion.16), channel_id=1, source_target_pairs={{0,2},{1,3},{2,0},{3,1},{4,6},{5,7},{6,4},{7,5},{8,10},{9,11},{10,... | collective-permute-start | bytes 442376 | tf_op jit(solution)/shard_map/ppermute | solution.py:384
  284.8 8.7 %collective-permute-start.53 = (bf16[2,24,768]{2,1,0:T(8,128)(2,1)S(1)}, bf16[2,24,768]{2,1,0:T(8,128)(2,1)S(1)}, u32[]{:S(2)}, u32[]{:S(2)}) collective-permute-start(bf16[2,24,768]{2,1,0:T(8,128)(2,1)S(1)} %dynamic-slice_bitcast_fusion.17), channel_id=1, source_target_pairs={{0,16},{4,20},{8,24},{12,28},{16,0},{20,4},{24,8},{28,12},{1,17},{... | collective-permute-start | bytes 221192 | tf_op jit(solution)/shard_map/ppermute | solution.py:384
  293.8 34.5 %collective-permute-start.54 = (bf16[24,768]{1,0:T(8,128)(2,1)S(1)}, bf16[24,768]{1,0:T(8,128)(2,1)S(1)}, u32[]{:S(2)}, u32[]{:S(2)}) collective-permute-start(bf16[24,768]{1,0:T(8,128)(2,1)S(1)} %dynamic-slice_bitcast_fusion.21), channel_id=1, source_target_pairs={{0,2},{1,3},{2,0},{3,1},{4,6},{5,7},{6,4},{7,5},{8,10},{9,11},{10,... | collective-permute-start | bytes 110600 | tf_op jit(solution)/shard_map/ppermute | solution.py:384
  302.7 24.2 %collective-permute-start.61 = (bf16[2,2,2,24,3072]{4,3,0,1,2:T(8,128)(2,1)S(1)}, bf16[2,2,2,24,3072]{4,3,0,1,2:T(8,128)(2,1)S(1)}, u32[]{:S(2)}, u32[]{:S(2)}) collective-permute-start(bf16[2,2,2,24,3072]{4,3,0,1,2:T(8,128)(2,1)S(1)} %dynamic-slice_bitcast_fusion), channel_id=1, source_target_pairs={{0,4},{4,0},{8,12},{12,8},{16,20},{20,16},{24,28},{28,24},{1,5},{5... | collective-permute-start | bytes 3538952 | tf_op jit(solution)/shard_map/ppermute | solution.py:384
  306.6 28.0 %collective-permute-start.56 = (bf16[2,2,2,96,768]{4,3,0,1,2:T(8,128)(2,1)S(1)}, bf16[2,2,2,96,768]{4,3,0,1,2:T(8,128)(2,1)S(1)}, u32[]{:S(2)}, u32[]{:S(2)}) collective-permute-start(bf16[2,2,2,96,768]{4,3,0,1,2:T(8,128)(2,1)S(1)} %dynamic-slice_bitcast_fusion.1), channel_id=1, source_target_pairs={{0,2},{1,3},{2,0},{3,1},{4,6},{5,7},{6,4},{7,5},{8,10},{9,11},{10,... | collective-permute-start | bytes 3538952 | tf_op jit(solution)/shard_map/ppermute | solution.py:384
  327.3 15.3 %collective-permute-start.62 = (bf16[2,2,24,3072]{3,2,0,1:T(8,128)(2,1)S(1)}, bf16[2,2,24,3072]{3,2,0,1:T(8,128)(2,1)S(1)}, u32[]{:S(2)}, u32[]{:S(2)}) collective-permute-start(bf16[2,2,24,3072]{3,2,0,1:T(8,128)(2,1)S(1)} %dynamic-slice_bitcast_fusion.2), channel_id=1, source_target_pairs={{0,2},{1,3},{2,0},{3,1},{4,6},{5,7},{6,4},{7,5},{8,10},{9,11},{10,... | collective-permute-start | bytes 1769480 | tf_op jit(solution)/shard_map/ppermute | solution.py:384
  334.9 9.9 %collective-permute-start.57 = (bf16[2,2,96,768]{3,2,0,1:T(8,128)(2,1)S(1)}, bf16[2,2,96,768]{3,2,0,1:T(8,128)(2,1)S(1)}, u32[]{:S(2)}, u32[]{:S(2)}) collective-permute-start(bf16[2,2,96,768]{3,2,0,1:T(8,128)(2,1)S(1)} %dynamic-slice_bitcast_fusion.3), channel_id=1, source_target_pairs={{0,4},{4,0},{8,12},{12,8},{16,20},{20,16},{24,28},{28,24},{1,5},{5... | collective-permute-start | bytes 1769480 | tf_op jit(solution)/shard_map/ppermute | solution.py:384
  342.8 9.2 %collective-permute-start.63 = (bf16[2,24,3072]{2,1,0:T(8,128)(2,1)S(1)}, bf16[2,24,3072]{2,1,0:T(8,128)(2,1)S(1)}, u32[]{:S(2)}, u32[]{:S(2)}) collective-permute-start(bf16[2,24,3072]{2,1,0:T(8,128)(2,1)S(1)} %dynamic-slice_bitcast_fusion.5), channel_id=1, source_target_pairs={{0,8},{4,12},{8,0},{12,4},{16,24},{20,28},{24,16},{28,20},{1,9},{5... | collective-permute-start | bytes 884744 | tf_op jit(solution)/shard_map/ppermute | solution.py:384
  345.1 12.7 %collective-permute-start.58 = (bf16[2,96,768]{2,1,0:T(8,128)(2,1)S(1)}, bf16[2,96,768]{2,1,0:T(8,128)(2,1)S(1)}, u32[]{:S(2)}, u32[]{:S(2)}) collective-permute-start(bf16[2,96,768]{2,1,0:T(8,128)(2,1)S(1)} %dynamic-slice_bitcast_fusion.6), channel_id=1, source_target_pairs={{0,8},{4,12},{8,0},{12,4},{16,24},{20,28},{24,16},{28,20},{1,9},{5... | collective-permute-start | bytes 884744 | tf_op jit(solution)/shard_map/ppermute | solution.py:384
  352.1 7.7 %collective-permute-start.64 = (bf16[24,3072]{1,0:T(8,128)(2,1)S(1)}, bf16[24,3072]{1,0:T(8,128)(2,1)S(1)}, u32[]{:S(2)}, u32[]{:S(2)}) collective-permute-start(bf16[24,3072]{1,0:T(8,128)(2,1)S(1)} %dynamic-slice_bitcast_fusion.11), channel_id=1, source_target_pairs={{0,16},{4,20},{8,24},{12,28},{16,0},{20,4},{24,8},{28,12},{1,17},{... | collective-permute-start | bytes 442376 | tf_op jit(solution)/shard_map/ppermute | solution.py:384
  (67 other events, 534.0 us)
